TPU v7x, 32 devices: a whole 2x2x4 slice. The times are simulated.
32 devices in a mesh: rep: 2 (over y), shard: 16 (over z, x, core).
Axes of the slice: x: 2, y: 2, z: 4, core: 2. Of those that a mesh axis runs over, the one named last changes fastest.
Arguments:
- tokens: bfloat16 [16384, 960], P(('rep', 'shard')), may hold values from -6 to 6
- segment_ids: int32 [32, 512], P(('rep', 'shard')), may hold values from 0 to 1, as said below
- positions: int32 [32, 512], P(('rep', 'shard')), may hold values from 0 to 1534, as said below
- norm_attn: bfloat16 [960], P('shard'), may hold values from 0.099609375 to 1.8984375
- w_qkv: bfloat16 [960, 1600], P('shard')
- w_out: bfloat16 [960, 960], P('shard'), may hold values from -0.5 to 0.5
- norm_mlp: bfloat16 [960], P('shard'), may hold values from 0.099609375 to 1.8984375
- w_gate_up: bfloat16 [960, 5120], P('shard'), may hold values from -0.1875 to 0.1875
- w_down: bfloat16 [2560, 960], P('shard'), may hold values from -0.25 to 0.25
- cotangent: bfloat16 [16384, 960], P(('rep', 'shard')), may hold values from -6 to 6
Outputs:
- output: bfloat16 [16384, 960], P(('rep', 'shard'))
- input_grad: float32 [16384, 960], P(('rep', 'shard'))
- grad_norm_attn: float32 [960], P('shard')
- grad_qkv: float32 [960, 1600], P('shard')
- grad_out: float32 [960, 960], P('shard')
- grad_norm_mlp: float32 [960], P('shard')
- grad_gate_up: float32 [960, 5120], P('shard')
- grad_down: float32 [2560, 960], P('shard')
Inputs may be any that keep to these rules, and one draw needn't show every extreme that they name: `segment_ids`: segment ids start at 0 in each sequence and rise by one at each new document; each sequence holds exactly 2 documents of one token or more. `positions`: a token's position within its document; the first document of a sequence starts at a position of 0 to 1024, every other document at 0.
All inputs are finite; a program needn't handle non-finite values.
Results may differ from a plain program's by a relative error of at most 0.015.
Values may be sent and summed in bfloat16 or wider, within the bound.
No kernel may reach another device: no remote copies, remote signals or barrier semaphores. Data moves between devices by JAX's collectives and lax.ppermute only.
A program may use at most 128 MiB of HBM per device.

v0:
```python
import jax
import jax.numpy as jnp
from jax import lax
from jax.sharding import PartitionSpec as P

HEADS = 15
KV_HEADS = 5
HD = 64


EPSILON = 1e-05
ROPE_BASE = 100000.0
NEG_FILL = -1e30


def rope_tables(places):
    half_dim = HD // 2
    freqs = ROPE_BASE ** (-2.0 * jnp.arange(half_dim, dtype=jnp.float32) / HD)
    angles = places.astype(jnp.float32)[..., None] * freqs
    return (jnp.cos(angles), jnp.sin(angles))


def rotate(values, cosine, sine):
    half_dim = values.shape[-1] // 2
    cosine = cosine[..., None, :]
    sine = sine[..., None, :]
    first_half = values[..., :half_dim]
    second_half = values[..., half_dim:]
    return jnp.concatenate(
        [first_half * cosine - second_half * sine, second_half * cosine + first_half * sine], -1
    )


def unrotate(grads, cosine, sine):
    half_dim = grads.shape[-1] // 2
    cosine = cosine[..., None, :]
    sine = sine[..., None, :]
    first_half = grads[..., :half_dim]
    second_half = grads[..., half_dim:]
    return jnp.concatenate(
        [first_half * cosine + second_half * sine, second_half * cosine - first_half * sine], -1
    )


def norm_forward(values, gain):
    scale = lax.rsqrt(jnp.mean(values * values, -1, keepdims=True) + EPSILON)
    return (values * scale * gain, scale)


def norm_backward(values, scale, gain, grads):
    weighted = grads * gain
    values_grad = scale * weighted - values * (scale * scale * scale) * jnp.mean(
        weighted * values, -1, keepdims=True
    )
    gain_grad = jnp.sum(grads * values * scale, 0)
    return (values_grad, gain_grad)


def block_mask(seg_row, start, block_rows):
    seq_len = seg_row.shape[0]
    rows = start + jnp.arange(block_rows, dtype=jnp.int32)
    places = jnp.arange(seq_len, dtype=jnp.int32)
    return (seg_row[:, None] == seg_row[None, :]) & (places[None, :] <= rows[:, None])


def block_scores(query_block, key_low, allowed):
    scores = (
        jnp.einsum("bkge,mke->kgbm", query_block, key_low, preferred_element_type=jnp.float32)
        * 0.125
    )
    return jnp.where(allowed[None, None], scores, NEG_FILL)


def per_device(
    tokens, segment_ids, positions, norm_attn, w_qkv, w_out, norm_mlp, w_gate_up, w_down, cotangent
):
    seq_len, model_width = tokens.shape
    hidden_units = w_gate_up.shape[1] // 2
    kv_width = KV_HEADS * HD
    group_size = HEADS // KV_HEADS
    block_rows = min(512, seq_len)
    num_blocks = seq_len // block_rows
    inputs = tokens.astype(jnp.float32)
    qkv_full, out_full, gain_attn, gain_mlp = (
        lax.all_gather(w_qkv, "shard", axis=0, tiled=True),
        lax.all_gather(w_out, "shard", axis=0, tiled=True),
        lax.all_gather(norm_attn, "shard", axis=0, tiled=True),
        lax.all_gather(norm_mlp, "shard", axis=0, tiled=True),
    )
    gain_attn = gain_attn.astype(jnp.float32)
    gain_mlp = gain_mlp.astype(jnp.float32)
    normed, scale_attn = norm_forward(inputs, gain_attn)
    normed_low = normed.astype(jnp.bfloat16)
    project = jnp.dot(normed_low, qkv_full, preferred_element_type=jnp.float32)
    cosine, sine = rope_tables(positions[0])
    query_low = rotate(project[:, :model_width].reshape(seq_len, HEADS, HD), cosine, sine).astype(
        jnp.bfloat16
    )
    key_low = rotate(
        project[:, model_width : model_width + kv_width].reshape(seq_len, KV_HEADS, HD),
        cosine,
        sine,
    ).astype(jnp.bfloat16)
    value_low = (
        project[:, model_width + kv_width :].reshape(seq_len, KV_HEADS, HD).astype(jnp.bfloat16)
    )
    seg_row = segment_ids[0]
    query_blocks = query_low.reshape(num_blocks, block_rows, KV_HEADS, group_size, HD)
    starts = jnp.arange(num_blocks, dtype=jnp.int32) * block_rows

    def attend(items):
        query_block, start = items
        allowed = block_mask(seg_row, start, block_rows)
        scores = block_scores(query_block, key_low, allowed)
        top_score = jnp.max(scores, -1, keepdims=True)
        expo = jnp.exp(scores - top_score)
        total_exp = jnp.sum(expo, -1, keepdims=True)
        log_total = top_score + jnp.log(total_exp)
        attn_prob = (expo / total_exp).astype(jnp.bfloat16)
        mixed = jnp.einsum(
            "kgbm,mke->bkge", attn_prob, value_low, preferred_element_type=jnp.float32
        )
        return (mixed.reshape(block_rows, model_width).astype(jnp.bfloat16), log_total)

    mixed_blocks, lse_blocks = lax.map(attend, (query_blocks, starts))
    mixed_low = mixed_blocks.reshape(seq_len, model_width)
    branch = jnp.dot(mixed_low, out_full, preferred_element_type=jnp.float32)
    after_attn = inputs + branch
    normed_mlp, scale_mlp = norm_forward(after_attn, gain_mlp)
    mlp_low = normed_mlp.astype(jnp.bfloat16)
    columns = mlp_low
    gate_up = jnp.dot(
        columns,
        lax.all_gather(w_gate_up, "shard", axis=0, tiled=True),
        preferred_element_type=jnp.float32,
    )
    gate = gate_up[:, :hidden_units]
    up_part = gate_up[:, hidden_units:]
    sigma = jax.nn.sigmoid(gate)
    activ = gate * sigma
    inner_low = (activ * up_part).astype(jnp.bfloat16)
    columns = inner_low
    mlp_branch = jnp.dot(
        columns,
        lax.all_gather(w_down, "shard", axis=0, tiled=True),
        preferred_element_type=jnp.float32,
    )
    output = (after_attn + mlp_branch).astype(jnp.bfloat16)
    cot_full = cotangent.astype(jnp.float32)
    inner_grad = jnp.einsum(
        "td,fd->tf",
        cotangent,
        lax.all_gather(w_down, "shard", axis=0, tiled=True),
        preferred_element_type=jnp.float32,
    )
    columns = inner_low
    grad_down = lax.psum_scatter(
        jnp.einsum("tf,td->fd", columns, cotangent, preferred_element_type=jnp.float32),
        "shard",
        scatter_dimension=0,
        tiled=True,
    )
    gate_grad = inner_grad * up_part * sigma * (1.0 + gate * (1.0 - sigma))
    up_grad = inner_grad * activ
    gate_up_grad = jnp.concatenate([gate_grad, up_grad], 1).astype(jnp.bfloat16)
    columns = mlp_low
    grad_gate_up = lax.psum_scatter(
        jnp.einsum("td,tf->df", columns, gate_up_grad, preferred_element_type=jnp.float32),
        "shard",
        scatter_dimension=0,
        tiled=True,
    )
    normed_mlp_grad = jnp.einsum(
        "tf,df->td",
        gate_up_grad,
        lax.all_gather(w_gate_up, "shard", axis=0, tiled=True),
        preferred_element_type=jnp.float32,
    )
    after_grad_norm, grad_gain_mlp = norm_backward(after_attn, scale_mlp, gain_mlp, normed_mlp_grad)
    after_grad = cot_full + after_grad_norm
    qkv_back, out_back = (
        lax.all_gather(w_qkv, "shard", axis=0, tiled=True),
        lax.all_gather(w_out, "shard", axis=0, tiled=True),
    )
    branch_grad = after_grad.astype(jnp.bfloat16)
    grad_out = jnp.einsum("ti,td->id", mixed_low, branch_grad, preferred_element_type=jnp.float32)
    mixed_grad = jnp.einsum(
        "td,id->ti", branch_grad, out_back, preferred_element_type=jnp.float32
    ).astype(jnp.bfloat16)
    grad_blocks = mixed_grad.reshape(num_blocks, block_rows, KV_HEADS, group_size, HD)

    def attend_back(carry, items):
        key_acc, value_acc = carry
        query_block, grad_block, lse_block, start = items
        allowed = block_mask(seg_row, start, block_rows)
        scores = block_scores(query_block, key_low, allowed)
        prob = jnp.exp(scores - lse_block)
        value_acc = value_acc + jnp.einsum(
            "kgbm,bkge->mke",
            prob.astype(jnp.bfloat16),
            grad_block,
            preferred_element_type=jnp.float32,
        )
        prob_grad = jnp.einsum(
            "bkge,mke->kgbm", grad_block, value_low, preferred_element_type=jnp.float32
        )
        row_dot = jnp.sum(prob * prob_grad, -1, keepdims=True)
        score_grad = (prob * (prob_grad - row_dot)).astype(jnp.bfloat16)
        query_part = (
            jnp.einsum("kgbm,mke->bkge", score_grad, key_low, preferred_element_type=jnp.float32)
            * 0.125
        )
        key_acc = (
            key_acc
            + jnp.einsum(
                "kgbm,bkge->mke", score_grad, query_block, preferred_element_type=jnp.float32
            )
            * 0.125
        )
        return ((key_acc, value_acc), query_part)

    empty_kv = jnp.zeros((seq_len, KV_HEADS, HD), jnp.float32)
    (key_grad, value_grad), query_parts = lax.scan(
        attend_back, (empty_kv, empty_kv), (query_blocks, grad_blocks, lse_blocks, starts)
    )
    query_grad = query_parts.reshape(seq_len, HEADS, HD)
    project_grad = jnp.concatenate(
        [
            unrotate(query_grad, cosine, sine).reshape(seq_len, model_width),
            unrotate(key_grad, cosine, sine).reshape(seq_len, kv_width),
            value_grad.reshape(seq_len, kv_width),
        ],
        1,
    ).astype(jnp.bfloat16)
    grad_qkv = jnp.einsum("ti,tj->ij", normed_low, project_grad, preferred_element_type=jnp.float32)
    normed_grad = jnp.einsum(
        "tj,ij->ti", project_grad, qkv_back, preferred_element_type=jnp.float32
    )
    input_grad_norm, grad_gain_attn = norm_backward(inputs, scale_attn, gain_attn, normed_grad)
    input_grad = after_grad + input_grad_norm
    shard_sums = (
        lax.psum_scatter(grad_qkv, "shard", scatter_dimension=0, tiled=True),
        lax.psum_scatter(grad_out, "shard", scatter_dimension=0, tiled=True),
        lax.psum_scatter(grad_gain_attn, "shard", scatter_dimension=0, tiled=True),
        lax.psum_scatter(grad_gain_mlp, "shard", scatter_dimension=0, tiled=True),
    )
    totals = (
        lax.psum(shard_sums[2].astype(jnp.bfloat16), "rep").astype(jnp.float32),
        lax.psum(shard_sums[0].astype(jnp.bfloat16), "rep").astype(jnp.float32),
        lax.psum(shard_sums[1].astype(jnp.bfloat16), "rep").astype(jnp.float32),
        lax.psum(shard_sums[3].astype(jnp.bfloat16), "rep").astype(jnp.float32),
        lax.psum(grad_gate_up.astype(jnp.bfloat16), "rep").astype(jnp.float32),
        lax.psum(grad_down.astype(jnp.bfloat16), "rep").astype(jnp.float32),
    )
    return (output, input_grad, totals[0], totals[1], totals[2], totals[3], totals[4], totals[5])


def solution(mesh):
    in_specs = (
        P(("rep", "shard"), None),
        P(("rep", "shard"), None),
        P(("rep", "shard"), None),
        P("shard"),
        P("shard", None),
        P("shard", None),
        P("shard"),
        P("shard", None),
        P("shard", None),
        P(("rep", "shard"), None),
    )
    out_specs = (
        P(("rep", "shard"), None),
        P(("rep", "shard"), None),
        P("shard"),
        P("shard", None),
        P("shard", None),
        P("shard"),
        P("shard", None),
        P("shard", None),
    )
    return jax.shard_map(
        per_device, mesh=mesh, in_specs=in_specs, out_specs=out_specs, check_vma=False
    )
```

profile of v0, /device:TPU:0, one launch (start us, length us, event | category | flops | bytes accessed | tf_op | source)
XLA Modules:
  0.0 823.3 jit_solution(5954537838803504254)
XLA Ops:
  7.9 0.7 all-gather.10.cloned.1.call-update
  8.7 0.7 all-gather.14.cloned.1.call-update
  10.0 1.4 fusion.51
  12.0 0.8 dynamic-update-slice
  12.9 0.8 dynamic-update-slice.1
  13.7 35.1 %all-reduce.11 = (bf16[960]{0:T(1024)(128)(2,1)S(1)}, bf16[960]{0:T(1024)(128)(2,1)S(1)}) all-reduce(bf16[960]{0:T(1024)(128)(2,1)S(1)} %dynamic-update-slice, bf16[960]{0:T(1024)(128)(2,1)S(1)} %dynamic-update-slice.1), channel_id=1, replica_groups=mesh['rep'=2,'shard'=16] {'shard'}, use_global_device_ids=true, to_apply=%add | all-reduce | flops 1920 | bytes 7680
  48.9 0.7 convert_element_type.111
  50.9 1.5 fusion.15
  53.3 1.0 fusion.33
  54.3 3.9 reshape.225
  58.2 43.7 %all-gather.10.cloned.1.call-done = bf16[16,60,1600]{2,1,0:T(8,128)(2,1)} async-done(((bf16[1,60,1600]{2,1,0:T(8,128)(2,1)}), bf16[16,60,1600]{2,1,0:T(8,128)(2,1)}) %all-gather.10.cloned.1.call-update) | async-done | bytes 3072016 | tf_op jit(solution)/shard_map/all_gather | solution.py:85
  101.9 4.8 reshape.223
  106.8 4.0 fusion.40
  111.5 7.0 fusion.52
  118.6 7.8 fusion.6
  126.4 7.3 fusion.24
  133.8 1.2 multiply_reduce_fusion.2
  135.1 56.0 %all-gather.14.cloned.1.call-done = bf16[16,60,5120]{2,1,0:T(8,128)(2,1)} async-done(((bf16[1,60,5120]{2,1,0:T(8,128)(2,1)}), bf16[16,60,5120]{2,1,0:T(8,128)(2,1)}) %all-gather.14.cloned.1.call-update) | async-done | bytes 9830416 | tf_op jit(solution)/shard_map/all_gather | solution.py:134
  191.1 10.6 %reshape.227 = bf16[960,5120]{1,0:T(8,128)(2,1)} reshape(bf16[16,60,5120]{2,1,0:T(8,128)(2,1)} %all-gather.14.cloned.1.call-done) | data formatting | bytes 19660800
  201.7 12.3 %fusion.49 = f32[512,5120]{1,0:T(8,128)} fusion(bf16[960,5120]{1,0:T(8,128)(2,1)} %reshape.227, f32[512,960]{0,1:T(8,128)S(1)} %get-tuple-element.102, f32[960]{0:T(1024)S(1)} %convert_element_type.117, f32[512]{0:T(512)S(1)} %get-tuple-element.95), kind=kOutput, calls=%fused_computation.95 | convolution fusion | flops 5034639360 | bytes 22288128 | tf_op jit(solution)/shard_map/dot_general | solution.py:132
  214.0 33.5 %all-gather.8.cloned.1.call-done = bf16[2560,960]{1,0:T(8,128)(2,1)} async-done(((bf16[160,960]{1,0:T(8,128)(2,1)}), bf16[2560,960]{1,0:T(8,128)(2,1)}) %all-gather.8.cloned.1.call-update) | async-done | bytes 4915216 | tf_op jit(solution)/shard_map/all_gather | solution.py:145
  247.4 10.9 %multiply_convert_fusion.1 = (bf16[512,2560]{1,0:T(8,128)(2,1)}, bf16[512,2560]{1,0:T(8,128)(2,1)}, bf16[512,2560]{1,0:T(8,128)(2,1)S(1)}) fusion(f32[512,5120]{1,0:T(8,128)} %fusion.49, bf16[512,960]{0,1:T(8,128)(2,1)} %param.19, bf16[2560,960]{1,0:T(8,128)(2,1)} %all-gather.8.cloned.1.call-done), kind=kOutput, calls=%fused_computation.16 | convolution fusion | flops 2536243200 | bytes 24248320 | tf_op jit(solution)/shard_map/td,fd->tf/dot_general | solution.py:150
  258.3 1.6 copy-done.30
  259.9 5.6 fusion.53
  265.6 12.5 %multiply_reduce_fusion = (f32[960]{0:T(1024)}, f32[512]{0:T(512)S(1)}, f32[512,960]{0,1:T(8,128)S(1)}) fusion(f32[512,960]{0,1:T(8,128)S(1)} %get-tuple-element.102, f32[512]{0:T(512)S(1)} %get-tuple-element.95, f32[960]{0:T(1024)S(1)} %convert_element_type.117, bf16[960,5120]{1,0:T(8,128)(2,1)} %reshape.227, bf16[512,2560]{1,0:T(8,128)(2,1)} %get-tuple-element.80, ...), kind=kOutput, calls=%fused_computation.37 | convolution fusion | flops 5046598144 | bytes 19017216 | tf_op jit(solution)/shard_map/tf,df->td/dot_general | solution.py:173
  278.0 2.5 subtract_add_fusion
  280.7 1.2 convolution_convert_fusion
  282.0 7.8 fusion.3
  289.8 7.7 fusion.5
  297.5 3.6 fusion.29
  301.2 0.8 pad_maximum_fusion.10
  302.0 2.5 convolution_multiply_fusion
  304.8 1.0 pad_maximum_fusion.5
  305.8 3.1 fusion.36
  309.0 3.0 fusion.30
  312.0 6.0 fusion.34
  318.0 9.7 %fusion.13 = f32[960,5120]{1,0:T(8,128)} fusion(bf16[512,2560]{1,0:T(8,128)(2,1)S(1)} %copy-done.33, bf16[512,2560]{1,0:T(8,128)(2,1)S(1)} %copy-done.32, f32[512,960]{0,1:T(8,128)S(1)} %copy-done.1, f32[960]{0:T(1024)S(1)} %convert_element_type.117, f32[512]{0:T(512)S(1)} %get-tuple-element.95), kind=kOutput, calls=%fused_computation.26 | convolution fusion | flops 5045125120 | bytes 26875648 | tf_op jit(solution)/shard_map/td,tf->df/dot_general | solution.py:168
  327.8 332.9 %fusion.50 = (f32[64,1600]{1,0:T(8,128)}, f32[64,960]{1,0:T(8,128)S(1)}, f32[64,5120]{1,0:T(8,128)S(1)}) fusion(f32[960,1600]{1,0:T(8,128)} %fusion.34, f32[960,960]{1,0:T(8,128)} %fusion.36, f32[960,5120]{1,0:T(8,128)} %fusion.13), kind=kCustom, calls=%all-reduce-scatter.3 | all-reduce-scatter fusion | flops 7864321 | bytes 31457792
  660.6 0.9 slice.68
  661.6 26.4 %collective-permute-start.2 = (bf16[60,5120]{1,0:T(8,128)(2,1)}, bf16[60,5120]{1,0:T(8,128)(2,1)}, u32[]{:S(2)}, u32[]{:S(2)}) collective-permute-start(bf16[60,5120]{1,0:T(8,128)(2,1)} %slice.68), channel_id=1, source_target_pairs={{0,1},{1,2},{2,3},{3,4},{4,5},{5,6},{6,7},{7,8},{8,9},{9,10},{10,1... | collective-permute-start | bytes 1843208
  688.0 6.6 fusion.23
  694.7 0.7 slice.66
  695.4 4.2 collective-permute-start
  700.3 1.9 collective-permute-start.1
  702.2 30.5 %all-reduce.10 = (bf16[960]{0:T(1024)(128)(2,1)}, bf16[960]{0:T(1024)(128)(2,1)}) all-reduce(f32[960]{0:T(1024)} %get-tuple-element.51, f32[960]{0:T(1024)S(1)} %copy-done.29), channel_id=2, replica_groups=mesh['rep'=2,'shard'=16] {'shard'}, use_global_device_ids=true, to_apply=%region_8.9.clone | all-reduce | flops 1920 | bytes 11520
  732.8 0.8 dynamic-slice.31
  733.5 1.3 dynamic-slice.30
  734.8 5.6 all-reduce.12
  740.4 1.2 convert_element_type.127
  741.6 1.1 convert_element_type.133
  742.7 3.0 concatenate.38
  745.7 1.6 dynamic-slice_convert_fusion.2
  747.3 4.2 concatenate.37
  751.5 1.7 dynamic-slice_convert_fusion.1
  753.2 8.0 concatenate.39
  761.2 2.2 dynamic-slice_convert_fusion
  763.4 1.9 convert_element_type.136
  765.3 3.5 fusion.20
  768.8 6.2 add_convert_fusion
  775.0 34.5 %all-reduce.17.cloned.1.call-done = (bf16[60,1600]{1,0:T(8,128)(2,1)}, bf16[60,960]{1,0:T(8,128)(2,1)}, bf16[60,5120]{1,0:T(8,128)(2,1)}, bf16[160,960]{1,0:T(8,128)(2,1)}) async-done(((bf16[60,1600]{1,0:T(8,128)(2,1)}, bf16[60,960]{1,0:T(8,128)(2,1)}, bf16[60,5120]{1,0:T(8,128)(2,1)}, bf16[160,960]{1,0:T(8,128)(2,1)}), (bf16[60,1600]{1,0:T(8,128)(2,1)}, bf16[60,960]{1,0:T(8,128)(2,1)}, ...) | async-done | bytes 1228816 | tf_op jit(solution)/shard_map/psum | solution.py:249
  809.5 1.8 convert_element_type.129
  811.2 1.6 convert_element_type.131
  812.9 2.2 convert_element_type.135
  815.1 0.9 convert_element_type.137
  (110 shorter events, 4.6 us)
Async XLA Ops:
  7.2 47.1 %all-gather.12.cloned.1.call-start = ((), (), s32[]{:S(2)}) async-start(), calls=%async_computation.4 | async-start | bytes 2228224 | tf_op jit(solution)/shard_map/all_gather | solution.py:86
  7.9 94.0 %all-gather.10.cloned.1.call-start = ((), (), s32[]{:S(2)}) async-start(), calls=%async_computation.3 | async-start | bytes 3620864 | tf_op jit(solution)/shard_map/all_gather | solution.py:85
  8.6 182.4 %all-gather.14.cloned.1.call-start = ((), (), s32[]{:S(2)}) async-start(), calls=%async_computation.5 | async-start | bytes 11141120 | tf_op jit(solution)/shard_map/all_gather | solution.py:134
  9.4 238.0 %all-gather.8.cloned.1.call-start = ((), (), s32[]{:S(2)}) async-start(), calls=%async_computation.1 | async-start | bytes 5570560 | tf_op jit(solution)/shard_map/all_gather | solution.py:145
  10.0 753.5 %reduce-scatter.8.cloned.1.call-start = ((), (), s32[]{:S(2)}) async-start(), calls=%async_computation.2 | async-start | bytes 11141120 | tf_op jit(solution)/shard_map/reduce_scatter | solution.py:157
  48.9 57.9 %copy-start.22 = (f32[960]{0:T(1024)}, f32[960]{0:T(1024)S(1)}, u32[]{:S(2)}) copy-start(f32[960]{0:T(1024)S(1)} %convert_element_type.108) | copy-start | bytes 11524
  53.0 53.8 %copy-start.26 = (f32[512]{0:T(512)}, f32[512]{0:T(512)S(1)}, u32[]{:S(2)}) copy-start(f32[512]{0:T(512)S(1)} %get-tuple-element.93) | copy-start | bytes 6148
  53.3 57.9 %copy-start.13 = (f32[512,32]{0,1:T(8,128)}, f32[512,32]{0,1:T(8,128)S(1)}, u32[]{:S(2)}) copy-start(f32[512,32]{0,1:T(8,128)S(1)} %get-tuple-element.91) | copy-start | bytes 196612
  58.2 48.5 %copy-start.3 = (bf16[512,960]{0,1:T(8,128)(2,1)S(1)}, bf16[512,960]{0,1:T(8,128)(2,1)}, u32[]{:S(2)}) copy-start(bf16[512,960]{0,1:T(8,128)(2,1)} %param.10) | copy-start | bytes 2949124
  111.1 7.4 copy-start.17
  111.2 7.4 copy-start.18
  111.5 7.1 copy-start.10
  111.5 7.1 copy-start.12
  126.4 7.4 copy-start.8
  133.7 1.3 copy-start.5
  135.0 130.5 %copy-start = (f32[512,960]{0,1:T(8,128)}, f32[512,960]{0,1:T(8,128)S(1)}, u32[]{:S(2)}) copy-start(f32[512,960]{0,1:T(8,128)S(1)} %get-tuple-element.102) | copy-start | bytes 5898244
  247.4 12.4 %copy-start.15 = (bf16[512,960]{0,1:T(8,128)(2,1)S(1)}, bf16[512,960]{0,1:T(8,128)(2,1)}, u32[]{:S(2)}) copy-start(bf16[512,960]{0,1:T(8,128)(2,1)} %param.19) | copy-start | bytes 2949124
  258.3 1.6 copy-start.30
  265.5 544.0 %all-reduce.17.cloned.1.call-start = ((), (), s32[]{:S(2)}) async-start(), calls=%async_computation.6 | async-start | bytes 2654208 | tf_op jit(solution)/shard_map/psum | solution.py:249
  265.5 12.5 %copy-start.16 = (bf16[512,960]{0,1:T(8,128)(2,1)S(1)}, bf16[512,960]{0,1:T(8,128)(2,1)}, u32[]{:S(2)}) copy-start(bf16[512,960]{0,1:T(8,128)(2,1)} %param.19) | copy-start | bytes 2949124
  265.5 16.3 %slice-start = ((s8[15728640]{0:T(1024)(128)(4,1)}), s8[4194304]{0:T(1024)(128)(4,1)S(1)}, s32[]{:S(2)}) async-start(s8[15728640]{0:T(1024)(128)(4,1)} %bitcast.88), calls=%async_computation.7 | async-start | bytes 8388608
  265.5 16.3 %slice-start.1 = ((s8[15728640]{0:T(1024)(128)(4,1)}), s8[4194304]{0:T(1024)(128)(4,1)S(1)}, s32[]{:S(2)}) async-start(s8[15728640]{0:T(1024)(128)(4,1)} %bitcast.88), calls=%async_computation.8 | async-start | bytes 8388608
  265.6 16.3 %slice-start.2 = ((s8[15728640]{0:T(1024)(128)(4,1)}), s8[4194304]{0:T(1024)(128)(4,1)S(1)}, s32[]{:S(2)}) async-start(s8[15728640]{0:T(1024)(128)(4,1)} %bitcast.88), calls=%async_computation.9 | async-start | bytes 8388608
  278.0 2.6 copy-start.9
  278.0 3.9 slice-start.3
  289.8 7.7 copy-start.11
  297.5 3.6 copy-start.14
  304.4 1.4 copy-start.6
  309.0 3.0 copy-start.19
  309.0 3.0 copy-start.23
  309.0 3.0 copy-start.27
  311.9 6.1 copy-start.21
  312.0 6.1 copy-start.1
  312.0 6.0 copy-start.32
  312.0 6.0 copy-start.33
  327.8 360.3 %copy-start.24 = (f32[960]{0:T(1024)S(1)}, f32[960]{0:T(1024)}, u32[]{:S(2)}) copy-start(f32[960]{0:T(1024)} %copy-done.22) | copy-start | bytes 11524
  327.8 360.3 %copy-start.28 = (f32[512]{0:T(512)S(1)}, f32[512]{0:T(512)}, u32[]{:S(2)}) copy-start(f32[512]{0:T(512)} %copy-done.26) | copy-start | bytes 6148
  661.6 33.1 %copy-start.7 = (f32[64,1600]{1,0:T(8,128)S(1)}, f32[64,1600]{1,0:T(8,128)}, u32[]{:S(2)}) copy-start(f32[64,1600]{1,0:T(8,128)} %get-tuple-element.76) | copy-start | bytes 1228804
  661.6 40.6 %copy-start.29 = (f32[960]{0:T(1024)S(1)}, f32[960]{0:T(1024)}, u32[]{:S(2)}) copy-start(f32[960]{0:T(1024)} %get-tuple-element.49) | copy-start | bytes 11524
  661.6 91.6 %collective-permute-start.2 = (bf16[60,5120]{1,0:T(8,128)(2,1)}, bf16[60,5120]{1,0:T(8,128)(2,1)}, u32[]{:S(2)}, u32[]{:S(2)}) collective-permute-start(bf16[60,5120]{1,0:T(8,128)(2,1)} %slice.68), channel_id=1, source_target_pairs={{0,1},{1,2},{2,3},{3,4},{4,5},{5,6},{6,7},{7,8},{8,9},{9,10},{10,1... | collective-permute-start | bytes 1843208
  695.4 51.9 %collective-permute-start = (bf16[60,1600]{1,0:T(8,128)(2,1)}, bf16[60,1600]{1,0:T(8,128)(2,1)}, u32[]{:S(2)}, u32[]{:S(2)}) collective-permute-start(bf16[60,1600]{1,0:T(8,128)(2,1)} %slice.66), channel_id=1, source_target_pairs={{0,1},{1,2},{2,3},{3,4},{4,5},{5,6},{6,7},{7,8},{8,9},{9,10},{10,1... | collective-permute-start | bytes 576008
  700.3 42.4 %collective-permute-start.1 = (bf16[60,960]{1,0:T(8,128)(2,1)}, bf16[60,960]{1,0:T(8,128)(2,1)}, u32[]{:S(2)}, u32[]{:S(2)}) collective-permute-start(bf16[60,960]{1,0:T(8,128)(2,1)} %slice.67), channel_id=1, source_target_pairs={{0,1},{1,2},{2,3},{3,4},{4,5},{5,6},{6,7},{7,8},{8,9},{9,10},{10,1... | collective-permute-start | bytes 345608
  761.2 4.1 copy-start.4
  761.2 4.1 copy-start.25
  765.3 3.5 copy-start.2
  765.3 3.5 copy-start.31
  809.5 5.6 copy-start.20
Sparse Core Ops, SparseCore 0:
  10.2 44.0 all-gather.11
  56.5 45.3 all-gather.9
  104.2 86.8 all-gather.13
  193.2 54.1 all-gather.7
  265.6 182.0 reduce-scatter.7
  765.4 44.0 all-reduce.16
where the time goes:
time: 834 us; the launch traced here: 823 us
  blocking collectives  404 us (48%)
  waiting for transfers between devices  170 us (20%)
  matrix products  111 us (13%)
  local copies, waits for them, and re-layouts  49.7 us (6%)
  other arithmetic  38.8 us (5%)
  starting transfers between devices  32.8 us (4%)
  between operations  17 us (2%)
    unnamed x3, blocking collectives  399 us
    all_gather x1, waiting for transfers between devices, per_device(): lax.all_gather(w_gate_up, 'shard', axis=0, tiled=True)  56 us
    unnamed x92, local copies, waits for them, and re-layouts  43.9 us
    all_gather x1, waiting for transfers between devices, per_device(): lax.all_gather(w_qkv, 'shard', axis=0, tiled=True)  43.7 us
    psum x1, waiting for transfers between devices, per_device(): lax.psum(shard_sums[0].astype(jnp.bfloat16), 'rep').astype(jnp.float32)  34.5 us
    all_gather x1, waiting for transfers between devices, per_device(): lax.all_gather(w_down, 'shard', axis=0, tiled=True)  33.5 us
    unnamed x3, starting transfers between devices  32.6 us
  transfers between devices with their start and end apart: 9, of which 4 were waited for; matrix products, arithmetic and copies ran while one was open for 61% of the time, Pallas kernels for 0%

commit v1 on v0

--- a/solution.py
+++ b/solution.py
@@ -1,3 +1,5 @@
+import functools
+
 import jax
 import jax.numpy as jnp
 from jax import lax
@@ -71,8 +73,198 @@
     return jnp.where(allowed[None, None], scores, NEG_FILL)
 
 
+AXES = ("rep", "shard")
+
+
+def hop(values, shards, move):
+    pairs = []
+    for rep in range(2):
+        for outer in range(shards // 4):
+            for mid in range(2):
+                for core in range(2):
+                    to = move(rep, outer, mid, core)
+                    pairs.append(
+                        (
+                            rep * shards + outer * 4 + mid * 2 + core,
+                            to[0] * shards + to[1] * 4 + to[2] * 2 + to[3],
+                        )
+                    )
+    return lax.ppermute(values, AXES, pairs)
+
+
+def core_move(rep, outer, mid, core):
+    return (rep, outer, mid, 1 - core)
+
+
+def rep_move(rep, outer, mid, core):
+    return (1 - rep, outer, mid, core)
+
+
+def first_move(rep, outer, mid, core):
+    return (rep, outer, 1 - mid, core) if core == 0 else (1 - rep, outer, mid, core)
+
+
+def second_move(rep, outer, mid, core):
+    return (1 - rep, outer, mid, core) if core == 0 else (rep, outer, 1 - mid, core)
+
+
+def outer_move(step, count):
+    return lambda rep, outer, mid, core: (rep, (outer + step) % count, mid, core)
+
+
+def pick(array, index):
+    return lax.dynamic_index_in_dim(array, index, 0, keepdims=False)
+
+
+def place():
+    shard = lax.axis_index("shard")
+    return lax.axis_index("rep"), shard // 4, (shard // 2) % 2, shard % 2
+
+
+def gather_rows(block, shards):
+    rep, outer, mid, core = place()
+    count = shards // 4
+    rows, width = block.shape
+    part = width // 4
+    other = hop(
+        lax.dynamic_slice(block, (0, ((1 - core) * 2 + rep) * part), (rows, part)), shards, core_move
+    )
+    mine = lax.dynamic_slice(block, (0, (core * 2 + rep) * part), (rows, part))
+    both = jnp.stack([mine, other])
+    chip = jnp.concatenate([pick(both, core), pick(both, 1 - core)], 0)
+    held = jnp.stack([chip] + [hop(chip, shards, outer_move(k, count)) for k in range(1, count)])
+    held = jnp.stack([held, hop(held, shards, second_move)])
+    held = jnp.stack([held, hop(held, shards, first_move)])
+    swap = hop(held, shards, core_move)
+    halves = jnp.stack([held, swap])
+    columns = []
+    order = (outer - jnp.arange(count)) % count
+    for want_core in range(2):
+        half = pick(halves, core ^ want_core)
+        for want_rep in range(2):
+            pieces = []
+            for want_mid in range(2):
+                by_rep, by_mid = rep ^ want_rep, mid ^ want_mid
+                second = by_mid if want_core == 0 else by_rep
+                first = by_rep if want_core == 0 else by_mid
+                pieces.append(pick(half.reshape((4,) + half.shape[2:]), second * 2 + first))
+            quarter = jnp.stack(pieces, 1)
+            columns.append(jnp.concatenate([pick(quarter, order[k])[None] for k in range(count)], 0))
+    return jnp.concatenate([c.reshape(shards * rows, part) for c in columns], 1)
+
+
+def add_low(*terms):
+    total = terms[0].astype(jnp.float32)
+    for term in terms[1:]:
+        total = total + term.astype(jnp.float32)
+    return total.astype(jnp.bfloat16)
+
+
+def reduce_pieces(send_half, keep_half, piece, shards):
+    rep, outer, mid, core = place()
+    count = shards // 4
+    came = hop(send_half, shards, core_move)
+    first = core == 0
+    away = [(1 - mid, 0), (1 - mid, 1)], [(0, 1 - rep), (1, 1 - rep)]
+    stay = [(mid, 0), (mid, 1)], [(0, rep), (1, rep)]
+
+    def chosen(table, k):
+        return tuple(jnp.where(first, table[0][k][d], table[1][k][d]) for d in range(2))
+
+    def both(where):
+        return add_low(piece(keep_half, *where), piece(came, *where))
+
+    sent = jnp.stack([both(chosen(away, 0)), both(chosen(away, 1))])
+    got = hop(sent, shards, first_move)
+    last = jnp.where(first, rep, mid)
+
+    def held(k):
+        where = jnp.where(first, mid, k), jnp.where(first, k, rep)
+        return add_low(piece(keep_half, *where), piece(came, *where), pick(got, k))
+
+    got_last = hop(held(1 - last), shards, second_move)
+    where = (mid, rep)
+    mine = add_low(piece(keep_half, *where), piece(came, *where), pick(got, last), got_last)
+    total = pick(mine, outer).astype(jnp.float32)
+    for k in range(1, count):
+        total = total + hop(
+            pick(mine, (outer + k) % count), shards, outer_move(k, count)
+        ).astype(jnp.float32)
+    return total.astype(jnp.bfloat16)
+
+
+def reduce_columns(grad, shards):
+    core = place()[3]
+    rows, width = grad.shape
+    half, part = width // 2, width // 4
+    count = shards // 4
+
+    def piece(array, mid, rep):
+        array = array.reshape(count, 2, rows // (2 * count), half)
+        out = lax.dynamic_slice(
+            array, (0, mid, 0, rep * part), (count, 1, rows // (2 * count), part)
+        )
+        return out[:, 0]
+
+    return reduce_pieces(
+        lax.dynamic_slice(grad, (0, (1 - core) * half), (rows, half)),
+        lax.dynamic_slice(grad, (0, core * half), (rows, half)),
+        piece,
+        shards,
+    )
+
+
+def reduce_rows(grad, shards):
+    core = place()[3]
+    rows, width = grad.shape
+    count = shards // 4
+    part = rows // (2 * shards)
+    blocks = grad.reshape(count, 2, 2, 2, part, width)
+
+    def half(which):
+        return lax.dynamic_slice(
+            blocks, (0, 0, which, 0, 0, 0), (count, 2, 1, 2, part, width)
+        )[:, :, 0]
+
+    def piece(array, mid, rep):
+        return lax.dynamic_slice(array, (0, mid, rep, 0, 0), (count, 1, 1, part, width))[:, 0, 0]
+
+    return reduce_pieces(half(1 - core), half(core), piece, shards)
+
+
+def share_columns(total, shards):
+    rep, outer, mid, core = place()
+    rows = total.shape[0] // 2
+
+    def rows_of(which):
+        return lax.dynamic_slice(total, (which * rows, 0), (rows, total.shape[1]))
+
+    parts = [
+        rows_of(core),
+        hop(rows_of(core), shards, rep_move),
+        hop(rows_of(1 - core), shards, core_move),
+        hop(rows_of(1 - core), shards, lambda r, o, m, c: (1 - r, o, m, 1 - c)),
+    ]
+    stack = jnp.stack(parts)
+    return [pick(stack, q ^ (core * 2 + rep)) for q in range(4)]
+
+
+def share_rows(total, shards):
+    rep = place()[0]
+    stack = jnp.stack([total, hop(total, shards, rep_move)])
+    return jnp.concatenate([pick(stack, rep), pick(stack, 1 - rep)], 0)
+
+
+def spread(features, shards):
+    rows = features // shards
+    padded = -(-rows // 8) * 8
+    at = jnp.arange(features)
+    target = at // rows * padded + at % rows
+    return (target[:, None] == jnp.arange(padded * shards)[None, :]).astype(jnp.bfloat16)
+
+
 def per_device(
-    tokens, segment_ids, positions, norm_attn, w_qkv, w_out, norm_mlp, w_gate_up, w_down, cotangent
+    shards, tokens, segment_ids, positions, norm_attn, w_qkv, w_out, norm_mlp, w_gate_up, w_down, cotangent
 ):
     seq_len, model_width = tokens.shape
     hidden_units = w_gate_up.shape[1] // 2
@@ -81,12 +273,27 @@
     block_rows = min(512, seq_len)
     num_blocks = seq_len // block_rows
     inputs = tokens.astype(jnp.float32)
-    qkv_full, out_full, gain_attn, gain_mlp = (
-        lax.all_gather(w_qkv, "shard", axis=0, tiled=True),
-        lax.all_gather(w_out, "shard", axis=0, tiled=True),
-        lax.all_gather(norm_attn, "shard", axis=0, tiled=True),
-        lax.all_gather(norm_mlp, "shard", axis=0, tiled=True),
-    )
+    tail = (-(w_qkv.shape[1] - kv_width * 2)) % 128
+    edge = model_width - tail
+    head = model_width + tail
+    mixed_block = jnp.concatenate(
+        [w_qkv[:, :model_width], w_out[:, edge:], w_qkv[:, model_width:], w_out[:, :edge]], 1
+    )
+    mixed_full = gather_rows(mixed_block, shards)
+    qkv_full = jnp.concatenate(
+        [mixed_full[:, :model_width], mixed_full[:, head : head + 2 * kv_width]], 1
+    )
+    out_full = jnp.concatenate(
+        [mixed_full[:, head + 2 * kv_width :], mixed_full[:, model_width:head]], 1
+    )
+    pad_rows = (-w_gate_up.shape[0]) % 8
+    gate_up_full = lax.all_gather(
+        jnp.pad(w_gate_up, ((0, pad_rows), (0, 0))), "shard", axis=0, tiled=True
+    )
+    down_full = lax.all_gather(w_down, "shard", axis=0, tiled=True)
+    spreader = spread(model_width, shards)
+    gains = lax.all_gather(jnp.stack([norm_attn, norm_mlp]), "shard", axis=1, tiled=True)
+    gain_attn, gain_mlp = gains[0], gains[1]
     gain_attn = gain_attn.astype(jnp.float32)
     gain_mlp = gain_mlp.astype(jnp.float32)
     normed, scale_attn = norm_forward(inputs, gain_attn)
@@ -129,9 +336,10 @@
     normed_mlp, scale_mlp = norm_forward(after_attn, gain_mlp)
     mlp_low = normed_mlp.astype(jnp.bfloat16)
     columns = mlp_low
+    mlp_spread = jnp.dot(mlp_low, spreader, preferred_element_type=jnp.float32).astype(jnp.bfloat16)
     gate_up = jnp.dot(
-        columns,
-        lax.all_gather(w_gate_up, "shard", axis=0, tiled=True),
+        mlp_spread,
+        gate_up_full,
         preferred_element_type=jnp.float32,
     )
     gate = gate_up[:, :hidden_units]
@@ -142,7 +350,7 @@
     columns = inner_low
     mlp_branch = jnp.dot(
         columns,
-        lax.all_gather(w_down, "shard", axis=0, tiled=True),
+        down_full,
         preferred_element_type=jnp.float32,
     )
     output = (after_attn + mlp_branch).astype(jnp.bfloat16)
@@ -150,42 +358,36 @@
     inner_grad = jnp.einsum(
         "td,fd->tf",
         cotangent,
-        lax.all_gather(w_down, "shard", axis=0, tiled=True),
+        down_full,
         preferred_element_type=jnp.float32,
     )
     columns = inner_low
-    grad_down = lax.psum_scatter(
-        jnp.einsum("tf,td->fd", columns, cotangent, preferred_element_type=jnp.float32),
-        "shard",
-        scatter_dimension=0,
-        tiled=True,
-    )
+    grad_down = jnp.einsum(
+        "tf,td->fd", columns, cotangent, preferred_element_type=jnp.float32
+    ).astype(jnp.bfloat16)
+    grad_down = reduce_rows(grad_down, shards)
     gate_grad = inner_grad * up_part * sigma * (1.0 + gate * (1.0 - sigma))
     up_grad = inner_grad * activ
     gate_up_grad = jnp.concatenate([gate_grad, up_grad], 1).astype(jnp.bfloat16)
     columns = mlp_low
-    grad_gate_up = lax.psum_scatter(
-        jnp.einsum("td,tf->df", columns, gate_up_grad, preferred_element_type=jnp.float32),
-        "shard",
-        scatter_dimension=0,
-        tiled=True,
-    )
+    grad_gate_up = jnp.einsum(
+        "td,tf->df", columns, gate_up_grad, preferred_element_type=jnp.float32
+    ).astype(jnp.bfloat16)
+    grad_gate_up = reduce_columns(grad_gate_up, shards)
+    spread_grad = jnp.einsum(
+        "tf,df->td", gate_up_grad, gate_up_full, preferred_element_type=jnp.float32
+    )
+    grad_high = spread_grad.astype(jnp.bfloat16)
+    grad_rest = (spread_grad - grad_high.astype(jnp.float32)).astype(jnp.bfloat16)
     normed_mlp_grad = jnp.einsum(
-        "tf,df->td",
-        gate_up_grad,
-        lax.all_gather(w_gate_up, "shard", axis=0, tiled=True),
-        preferred_element_type=jnp.float32,
-    )
+        "tp,dp->td", grad_high, spreader, preferred_element_type=jnp.float32
+    ) + jnp.einsum("tp,dp->td", grad_rest, spreader, preferred_element_type=jnp.float32)
     after_grad_norm, grad_gain_mlp = norm_backward(after_attn, scale_mlp, gain_mlp, normed_mlp_grad)
     after_grad = cot_full + after_grad_norm
-    qkv_back, out_back = (
-        lax.all_gather(w_qkv, "shard", axis=0, tiled=True),
-        lax.all_gather(w_out, "shard", axis=0, tiled=True),
-    )
     branch_grad = after_grad.astype(jnp.bfloat16)
     grad_out = jnp.einsum("ti,td->id", mixed_low, branch_grad, preferred_element_type=jnp.float32)
     mixed_grad = jnp.einsum(
-        "td,id->ti", branch_grad, out_back, preferred_element_type=jnp.float32
+        "td,id->ti", branch_grad, out_full, preferred_element_type=jnp.float32
     ).astype(jnp.bfloat16)
     grad_blocks = mixed_grad.reshape(num_blocks, block_rows, KV_HEADS, group_size, HD)
 
@@ -234,25 +436,44 @@
     ).astype(jnp.bfloat16)
     grad_qkv = jnp.einsum("ti,tj->ij", normed_low, project_grad, preferred_element_type=jnp.float32)
     normed_grad = jnp.einsum(
-        "tj,ij->ti", project_grad, qkv_back, preferred_element_type=jnp.float32
+        "tj,ij->ti", project_grad, qkv_full, preferred_element_type=jnp.float32
     )
     input_grad_norm, grad_gain_attn = norm_backward(inputs, scale_attn, gain_attn, normed_grad)
     input_grad = after_grad + input_grad_norm
-    shard_sums = (
-        lax.psum_scatter(grad_qkv, "shard", scatter_dimension=0, tiled=True),
-        lax.psum_scatter(grad_out, "shard", scatter_dimension=0, tiled=True),
-        lax.psum_scatter(grad_gain_attn, "shard", scatter_dimension=0, tiled=True),
-        lax.psum_scatter(grad_gain_mlp, "shard", scatter_dimension=0, tiled=True),
-    )
-    totals = (
-        lax.psum(shard_sums[2].astype(jnp.bfloat16), "rep").astype(jnp.float32),
-        lax.psum(shard_sums[0].astype(jnp.bfloat16), "rep").astype(jnp.float32),
-        lax.psum(shard_sums[1].astype(jnp.bfloat16), "rep").astype(jnp.float32),
-        lax.psum(shard_sums[3].astype(jnp.bfloat16), "rep").astype(jnp.float32),
-        lax.psum(grad_gate_up.astype(jnp.bfloat16), "rep").astype(jnp.float32),
-        lax.psum(grad_down.astype(jnp.bfloat16), "rep").astype(jnp.float32),
-    )
-    return (output, input_grad, totals[0], totals[1], totals[2], totals[3], totals[4], totals[5])
+    grad_mixed = jnp.concatenate(
+        [
+            grad_qkv[:, :model_width],
+            grad_out[:, edge:],
+            grad_qkv[:, model_width:],
+            grad_out[:, :edge],
+        ],
+        1,
+    ).astype(jnp.bfloat16)
+    grad_mixed = reduce_columns(grad_mixed, shards)
+    part = grad_mixed.shape[1]
+    quarters = share_columns(jnp.concatenate([grad_mixed, grad_gate_up], 1), shards)
+    whole_mixed = jnp.concatenate([q[:, :part] for q in quarters], 1).astype(jnp.float32)
+    whole_gate_up = jnp.concatenate([q[:, part:] for q in quarters], 1).astype(jnp.float32)
+    whole_qkv = jnp.concatenate(
+        [whole_mixed[:, :model_width], whole_mixed[:, head : head + 2 * kv_width]], 1
+    )
+    whole_out = jnp.concatenate(
+        [whole_mixed[:, head + 2 * kv_width :], whole_mixed[:, model_width:head]], 1
+    )
+    whole_down = share_rows(grad_down, shards).astype(jnp.float32)
+    gain_grads = lax.psum(jnp.stack([grad_gain_attn, grad_gain_mlp]), AXES)
+    rows = model_width // shards
+    gain_grads = lax.dynamic_slice(gain_grads, (0, lax.axis_index("shard") * rows), (2, rows))
+    return (
+        output,
+        input_grad,
+        gain_grads[0],
+        whole_qkv,
+        whole_out,
+        gain_grads[1],
+        whole_gate_up,
+        whole_down,
+    )
 
 
 def solution(mesh):
@@ -279,5 +500,5 @@
         P("shard", None),
     )
     return jax.shard_map(
-        per_device, mesh=mesh, in_specs=in_specs, out_specs=out_specs, check_vma=False
-    )
+        functools.partial(per_device, mesh.shape["shard"]), mesh=mesh, in_specs=in_specs, out_specs=out_specs, check_vma=False
+    )

time: 834 us -> 490 us (0.59)
  blocking collectives: 404 us -> 90.2 us
  waiting for transfers between devices: 170 us -> 127 us
  other arithmetic: 38.8 us -> 57.1 us
    unnamed x3 -> x0, blocking collectives: 399 us -> none
    all_gather x4 -> x2, waiting for transfers between devices: 133 us -> 6.33 us  [the longest x1 6.31 us: per_device(): down_full = lax.all_gather(w_down, 'shard', axis=0, tiled=True)]
    ppermute x0 -> x29, waiting for transfers between devices: none -> 121 us  [hop(): return lax.ppermute(values, AXES, pairs)]
    psum x1, blocking collectives: 5.58 us -> 56.3 us  [per_device(): gain_grads = lax.psum(jnp.stack([grad_gain_attn, grad_gain_mlp]), AXES)]
    ppermute x0 -> x29, starting transfers between devices: none -> 34.5 us  [hop(): return lax.ppermute(values, AXES, pairs)]
    psum x1 -> x0, waiting for transfers between devices: 34.5 us -> none  [per_device(): lax.psum(shard_sums[0].astype(jnp.bfloat16), 'rep').astype(jnp.float32)]
    all_gather x0 -> x1, blocking collectives: none -> 34 us  [per_device(): lax.all_gather(jnp.stack([norm_attn, norm_mlp]), 'shard', axis=1, tiled=T...]
    unnamed x92 -> x125, local copies, waits for them, and re-layouts: 43.9 us -> 10.1 us
  transfers between devices with their start and end apart: 9 -> 31, of which waited for: 4 -> 12; matrix products, arithmetic and copies ran while one was open for 61% -> 29% of each run, Pallas kernels for 0% -> 0%
where the time goes in v1:
time: 490 us; the launch traced here: 485 us
  waiting for transfers between devices  127 us (26%)
  matrix products  103 us (21%)
  blocking collectives  90.2 us (18%)
  other arithmetic  57.1 us (12%)
  local copies, waits for them, and re-layouts  49.3 us (10%)
  starting transfers between devices  34.6 us (7%)
  between operations  23.8 us (5%)
    ppermute x29, waiting for transfers between devices, hop(): return lax.ppermute(values, AXES, pairs)  121 us
    psum x1, blocking collectives, per_device(): gain_grads = lax.psum(jnp.stack([grad_gain_attn, grad_gain_mlp]), AXES)  56.3 us
    ppermute x29, starting transfers between devices, hop(): return lax.ppermute(values, AXES, pairs)  34.5 us
    all_gather x1, blocking collectives, per_device(): lax.all_gather(jnp.stack([norm_attn, norm_mlp]), 'shard', axis=1, tiled=T...  34 us
    convert_element_type x9, other arithmetic, add_low(): return total.astype(jnp.bfloat16)  20.4 us
    dot_general x1, matrix products, per_device(): jnp.dot(mlp_spread, gate_up_full, preferred_element_type=jnp.float32)  14 us
    dot_general x1, matrix products, attend_back(): jnp.einsum('bkge,mke->kgbm', grad_block, value_low, preferred_element_typ...  12.7 us
    dynamic_slice x2, local copies, waits for them, and re-layouts, reduce_columns(): lax.dynamic_slice(grad, (0, core * half), (rows, half))  11 us
  transfers between devices with their start and end apart: 31, of which 12 were waited for; matrix products, arithmetic and copies ran while one was open for 29% of the time, Pallas kernels for 0%

profile of v1, /device:TPU:0, one launch (start us, length us, event | category | flops | bytes accessed | tf_op | source)
XLA Modules:
  0.0 485.3 jit_solution(6225942251097269296)
XLA Ops:
  7.3 2.0 pad.4
  11.2 4.0 collective-permute-start.2
  15.2 1.6 collective-permute-start.1
  16.8 2.2 collective-permute-start.3
  19.1 9.0 %collective-permute-done.2 = bf16[120,640]{1,0:T(8,128)(2,1)S(1)} collective-permute-done((bf16[120,640]{1,0:T(8,128)(2,1)S(1)}, bf16[120,640]{1,0:T(8,128)(2,1)S(1)}, u32[]{:S(2)}, u32[]{:S(2)}) %collective-permute-start.2) | collective-permute-done | bytes 153632 | tf_op jit(solution)/shard_map/ppermute | solution.py:92
  28.1 4.0 collective-permute-done.3
  32.2 1.7 collective-permute-start.4
  34.0 9.7 %collective-permute-done.4 = bf16[4,120,640]{2,1,0:T(8,128)(2,1)S(1)} collective-permute-done((bf16[4,120,640]{2,1,0:T(8,128)(2,1)S(1)}, bf16[4,120,640]{2,1,0:T(8,128)(2,1)S(1)}, u32[]{:S(2)}, u32[]{:S(2)}) %collective-permute-start.4) | collective-permute-done | bytes 614432 | tf_op jit(solution)/shard_map/ppermute | solution.py:92
  43.9 3.0 collective-permute-start.5
  46.9 21.7 %collective-permute-done.5 = bf16[2,4,120,640]{3,2,1,0:T(8,128)(2,1)S(1)} collective-permute-done((bf16[2,4,120,640]{3,2,1,0:T(8,128)(2,1)S(1)}, bf16[2,4,120,640]{3,2,1,0:T(8,128)(2,1)S(1)}, u32[]{:S(2)}, u32[]{:S(2)}) %collective-permute-start.5) | collective-permute-done | bytes 1228832 | tf_op jit(solution)/shard_map/ppermute | solution.py:92
  68.6 1.9 pad_maximum_fusion.3
  76.7 34.0 %all-gather = bf16[16,60,2]{1,2,0:T(2,128)(2,1)S(1)} all-gather(bf16[1,60,2]{1,2,0:T(2,128)(2,1)S(1)} %maximum_bitcast_fusion.3), channel_id=1, replica_groups=mesh['rep'=2,'shard'=16] {'shard'}, dimensions={0}, use_global_device_ids=true | all-gather | bytes 4080 | tf_op jit(solution)/shard_map/all_gather | solution.py:295
  115.0 3.8 fusion.20
  120.8 2.7 fusion.94
  123.6 1.7 copy-done.2
  127.9 6.9 %fusion.131 = (f32[5,3,512]{2,1,0:T(4,128)S(1)}, f32[5,3,512,512]{2,3,1,0:T(8,128)}) fusion(bf16[512,5,3,32]{0,3,2,1:T(8,128)(2,1)S(1)} %bitcast.303, bf16[512,5,3,32]{0,3,2,1:T(8,128)(2,1)S(1)} %bitcast.301, bf16[512,5,32]{0,2,1:T(8,128)(2,1)S(1)} %get-tuple-element.120, bf16[512,5,32]{0,2,1:T(8,128)(2,1)S(1)} %get-tuple-element.119, ...), kind=kOutput, calls=%fused_computation.306 | convolution fusion | flops 517726720 | bytes 17332224 | tf_op jit(solution)/shard_map/while/body/eval_jaxpr/bkge,mke->kgbm/dot_general | solution.py:70
  134.9 7.8 %fusion.3 = f32[5,3,512]{2,1,0:T(4,128)S(1)} fusion(f32[5,3,512,512]{2,3,1,0:T(8,128)} %get-tuple-element.152, f32[5,3,512]{2,1,0:T(4,128)S(1)} %get-tuple-element.151), kind=kLoop, calls=%fused_computation.9 | loop fusion | flops 7856640 | bytes 15790080 | tf_op jit(solution)/shard_map/while/body/eval_jaxpr/reduce_sum | solution.py:324
  142.7 8.0 %fusion.39 = bf16[5,64,3,512]{3,1,2,0:T(8,128)(2,1)S(1)} fusion(bf16[512,5,64,1]{0,2,3,1:T(8,128)(2,1)S(1)} %bitcast.299, f32[5,3,512,512]{2,3,1,0:T(8,128)} %get-tuple-element.152, f32[5,3,512]{2,1,0:T(4,128)S(1)} %fusion.3, f32[5,3,512]{2,1,0:T(4,128)S(1)} %get-tuple-element.151), kind=kOutput, calls=%fused_computation.115 | convolution fusion | flops 515604480 | bytes 17100800 | tf_op jit(solution)/shard_map/while/body/eval_jaxpr/kgbm,mke->bkge/dot_general | solution.py:327
  152.1 14.0 %fusion.132 = f32[512,5120]{1,0:T(8,128)} fusion(bf16[1024,5120]{1,0:T(8,128)(2,1)} %all-gather.4.cloned.1.call-done, s32[960]{0:T(1024)S(1)} %fusion.113, f32[512,960]{0,1:T(8,128)S(1)} %get-tuple-element.154, f32[960]{0:T(1024)S(1)} %bitcast.334, f32[512]{0:T(512)S(1)} %get-tuple-element.144), kind=kOutput, calls=%fused_computation.307 | convolution fusion | flops 6378323968 | bytes 22947328 | tf_op jit(solution)/shard_map/dot_general | solution.py:340
  166.0 6.3 %all-gather.6.cloned.1.call-done = bf16[2560,960]{1,0:T(8,128)(2,1)} async-done(((bf16[160,960]{1,0:T(8,128)(2,1)}), bf16[2560,960]{1,0:T(8,128)(2,1)}) %all-gather.6.cloned.1.call-update) | async-done | bytes 4915216 | tf_op jit(solution)/shard_map/all_gather | solution.py:293
  172.3 10.2 %multiply_convert_fusion.1 = (bf16[512,2560]{1,0:T(8,128)(2,1)S(1)}, bf16[512,2560]{1,0:T(8,128)(2,1)}, bf16[512,2560]{1,0:T(8,128)(2,1)S(1)}) fusion(f32[512,5120]{1,0:T(8,128)} %fusion.132, bf16[512,960]{0,1:T(8,128)(2,1)S(1)} %copy-done.31, bf16[2560,960]{1,0:T(8,128)(2,1)} %all-gather.6.cloned.1.call-done), kind=kOutput, calls=%fused_computation.26 | convolution fusion | flops 2536243200 | bytes 24248320 | tf_op jit(solution)/shard_map/td,fd->tf/dot_general | solution.py:358
  182.6 10.6 %convolution_convert_fusion = bf16[960,5120]{1,0:T(8,128)(2,1)} fusion(bf16[512,2560]{1,0:T(8,128)(2,1)} %get-tuple-element.54, bf16[512,2560]{1,0:T(8,128)(2,1)S(1)} %get-tuple-element.53, f32[512,960]{0,1:T(8,128)S(1)} %get-tuple-element.154, f32[960]{0:T(1024)S(1)} %bitcast.335, f32[512]{0:T(512)S(1)} %get-tuple-element.144), kind=kOutput, calls=%fused_computation.11 | convolution fusion | flops 5050040320 | bytes 17045248 | tf_op jit(solution)/shard_map/td,tf->df/dot_general | solution.py:373
  193.2 9.7 %fusion.15 = f32[512,1024]{1,0:T(8,128)S(1)} fusion(bf16[1024,5120]{1,0:T(8,128)(2,1)} %all-gather.4.cloned.1.call-done, bf16[512,2560]{1,0:T(8,128)(2,1)} %get-tuple-element.54, bf16[512,2560]{1,0:T(8,128)(2,1)S(1)} %get-tuple-element.53), kind=kOutput, calls=%fused_computation.41 | convolution fusion | flops 5379194880 | bytes 17825792 | tf_op jit(solution)/shard_map/tf,df->td/dot_general | solution.py:377
  204.2 1.6 multiply_reduce_fusion
  205.9 2.2 subtract_add_fusion
  210.1 4.4 convolution_convert_fusion.1
  214.4 7.9 %copy.75 = bf16[2560,960]{1,0:T(8,128)(2,1)} copy(bf16[2560,960]{0,1:T(8,128)(2,1)} %convolution_convert_fusion.1) | data formatting | bytes 9830400 | tf_op jit(solution)/shard_map/convert_element_type | solution.py:367
  222.3 3.6 copy_bitcast_fusion
  226.1 8.1 %constant_dynamic-slice_fusion.2 = (bf16[960,2560]{1,0:T(8,128)(2,1)}, bf16[960,2560]{1,0:T(8,128)(2,1)}) fusion(bf16[960,5120]{1,0:T(8,128)(2,1)} %convolution_convert_fusion, s32[]{:T(128)S(6)} %select_n.442, s32[]{:T(128)S(6)} %select_n.444), kind=kLoop, calls=%fused_computation.257 | loop fusion | bytes 19660808 | tf_op jit(solution)/shard_map/dynamic_slice | solution.py:211
  234.6 12.7 %fusion = (f32[5,3,512]{2,1,0:T(4,128)S(1)}, f32[5,512,512,3]{2,1,3,0:T(8,128)}) fusion(f32[5,3,512,512]{2,3,1,0:T(8,128)} %get-tuple-element.152, f32[5,3,512]{2,1,0:T(4,128)S(1)} %log_add_fusion, bf16[512,5,64,1]{0,2,3,1:T(8,128)(2,1)S(1)} %bitcast.300, bf16[512,5,3,64]{0,3,2,1:T(8,128)(2,1)S(1)} %bitcast.294), kind=kOutput, calls=%fused_computation.2 | convolution fusion | flops 515105280 | bytes 32829440 | tf_op jit(solution)/shard_map/while/body/eval_jaxpr/bkge,mke->kgbm/dot_general | solution.py:406
  247.3 1.8 slice-done.2
  250.0 7.7 %fusion.2 = bf16[5,3,512,512]{2,3,1,0:T(8,128)(2,1)S(1)} fusion(f32[5,512,512,3]{2,1,3,0:T(8,128)} %get-tuple-element.157, f32[5,3,512,512]{2,3,1,0:T(8,128)S(1)} %bitcast.278, f32[5,3,512]{2,1,0:T(4,128)S(1)} %get-tuple-element.156, f32[5,3,512]{2,1,0:T(4,128)S(1)} %log_add_fusion), kind=kLoop, calls=%fused_computation.4 | loop fusion | flops 15728640 | bytes 39383040 | tf_op jit(solution)/shard_map/while/body/eval_jaxpr/convert_element_type | solution.py:410
  257.8 2.5 fusion.49
  260.4 2.6 convolution_multiply_fusion
  264.4 2.9 fusion.55
  267.4 3.3 convolution_convert_fusion.2
  275.3 7.3 %concatenate.104 = bf16[960,2560]{1,0:T(8,128)(2,1)} concatenate(bf16[960,960]{1,0:T(8,128)(2,1)S(1)} %slice.216, bf16[960,64]{1,0:T(8,128)(2,1)S(1)} %slice-done.6, bf16[960,640]{1,0:T(8,128)(2,1)S(1)} %slice.218, bf16[960,896]{1,0:T(8,128)(2,1)} %slice.219), dimensions={1} | concatenate | bytes 9830400 | tf_op jit(solution)/shard_map/concatenate | solution.py:443
  282.6 2.9 constant_dynamic-slice_fusion.4
  285.9 3.1 fusion.50
  291.3 2.3 fusion.32
  293.6 2.3 fusion.44
  297.4 1.8 fusion.29
  303.5 3.7 add_convert_fusion.2
  307.2 26.1 %collective-permute-done.23 = bf16[2,4,80,960]{3,2,1,0:T(8,128)(2,1)S(1)} collective-permute-done((bf16[2,4,80,960]{3,2,1,0:T(8,128)(2,1)S(1)}, bf16[2,4,80,960]{3,2,1,0:T(8,128)(2,1)S(1)}, u32[]{:S(2)}, u32[]{:S(2)}) %collective-permute-start.23) | collective-permute-done | bytes 1228832 | tf_op jit(solution)/shard_map/ppermute | solution.py:92
  333.3 2.9 fusion.40
  336.2 1.5 collective-permute-start.24
  337.7 4.1 fusion.21
  342.4 56.3 %psum.7 = f32[2,960]{1,0:T(2,128)S(1)} all-reduce(f32[2,960]{1,0:T(2,128)S(1)} %pad_maximum_fusion.26), channel_id=1, replica_groups=mesh['rep'=2,'shard'=16] {'rep','shard'}, use_global_device_ids=true, to_apply=%region_9.10 | all-reduce | flops 1920 | bytes 15360 | tf_op jit(solution)/shard_map/psum | solution.py:464
  398.7 1.6 fusion.52
  400.3 2.4 collective-permute-start.9
  403.3 1.8 fusion.42
  405.1 1.6 collective-permute-start.25
  406.7 2.3 collective-permute-start.27
  409.2 1.6 collective-permute-done.9
  410.8 1.6 fusion.54
  412.5 1.6 collective-permute-start.10
  414.1 2.5 collective-permute-start.12
  416.6 2.7 fusion.23
  419.3 2.8 collective-permute-start.11
  422.2 12.5 %collective-permute-done.26 = bf16[80,960]{1,0:T(8,128)(2,1)S(1)} collective-permute-done((bf16[80,960]{1,0:T(8,128)(2,1)S(1)}, bf16[80,960]{1,0:T(8,128)(2,1)S(1)}, u32[]{:S(2)}, u32[]{:S(2)}) %collective-permute-start.26) | collective-permute-done | bytes 153632 | tf_op jit(solution)/shard_map/ppermute | solution.py:92
  436.0 13.4 %collective-permute-done.11 = bf16[120,640]{1,0:T(8,128)(2,1)S(1)} collective-permute-done((bf16[120,640]{1,0:T(8,128)(2,1)S(1)}, bf16[120,640]{1,0:T(8,128)(2,1)S(1)}, u32[]{:S(2)}, u32[]{:S(2)}) %collective-permute-start.11) | collective-permute-done | bytes 153632 | tf_op jit(solution)/shard_map/ppermute | solution.py:92
  449.5 11.4 %collective-permute-done.17 = bf16[120,1280]{1,0:T(8,128)(2,1)S(1)} collective-permute-done((bf16[120,1280]{1,0:T(8,128)(2,1)S(1)}, bf16[120,1280]{1,0:T(8,128)(2,1)S(1)}, u32[]{:S(2)}, u32[]{:S(2)}) %collective-permute-start.17) | collective-permute-done | bytes 307232 | tf_op jit(solution)/shard_map/ppermute | solution.py:92
  461.3 1.7 collective-permute-start.21
  464.5 10.4 %collective-permute-done.19 = bf16[60,1920]{1,0:T(8,128)(2,1)S(1)} collective-permute-done((bf16[60,1920]{1,0:T(8,128)(2,1)S(1)}, bf16[60,1920]{1,0:T(8,128)(2,1)S(1)}, u32[]{:S(2)}, u32[]{:S(2)}) %collective-permute-start.19) | collective-permute-done | bytes 230432 | tf_op jit(solution)/shard_map/ppermute | solution.py:92
  (260 shorter events, 37.3 us)
Async XLA Ops:
  7.2 144.9 %all-gather.4.cloned.1.call-start = ((), (), s32[]{:S(2)}) async-start(), calls=%async_computation | async-start | bytes 11141120 | tf_op jit(solution)/shard_map/all_gather | solution.py:290
  9.3 163.0 %all-gather.6.cloned.1.call-start = ((), (), s32[]{:S(2)}) async-start(), calls=%async_computation.1 | async-start | bytes 5570560 | tf_op jit(solution)/shard_map/all_gather | solution.py:293
  9.7 1.4 collective-permute-start
  11.2 16.9 %collective-permute-start.2 = (bf16[120,640]{1,0:T(8,128)(2,1)S(1)}, bf16[120,640]{1,0:T(8,128)(2,1)S(1)}, u32[]{:S(2)}, u32[]{:S(2)}) collective-permute-start(bf16[120,640]{1,0:T(8,128)(2,1)S(1)} %pad_maximum_fusion.25), channel_id=1, source_target_pairs={{0,8},{1,9},{2,10},{3,11},{4,12},{5,13},{6,14},{7,15},{8,0},{9,1},... | collective-permute-start | bytes 460808 | tf_op jit(solution)/shard_map/ppermute | solution.py:92
  15.2 12.9 %collective-permute-start.1 = (bf16[120,640]{1,0:T(8,128)(2,1)S(1)}, bf16[120,640]{1,0:T(8,128)(2,1)S(1)}, u32[]{:S(2)}, u32[]{:S(2)}) collective-permute-start(bf16[120,640]{1,0:T(8,128)(2,1)S(1)} %pad_maximum_fusion.25), channel_id=1, source_target_pairs={{0,4},{1,5},{2,6},{3,7},{4,8},{5,9},{6,10},{7,11},{8,12},{9,13},{1... | collective-permute-start | bytes 460808 | tf_op jit(solution)/shard_map/ppermute | solution.py:92
  16.8 15.3 %collective-permute-start.3 = (bf16[120,640]{1,0:T(8,128)(2,1)S(1)}, bf16[120,640]{1,0:T(8,128)(2,1)S(1)}, u32[]{:S(2)}, u32[]{:S(2)}) collective-permute-start(bf16[120,640]{1,0:T(8,128)(2,1)S(1)} %pad_maximum_fusion.25), channel_id=1, source_target_pairs={{0,12},{1,13},{2,14},{3,15},{4,0},{5,1},{6,2},{7,3},{8,4},{9,5},{1... | collective-permute-start | bytes 460808 | tf_op jit(solution)/shard_map/ppermute | solution.py:92
  32.2 11.5 %collective-permute-start.4 = (bf16[4,120,640]{2,1,0:T(8,128)(2,1)S(1)}, bf16[4,120,640]{2,1,0:T(8,128)(2,1)S(1)}, u32[]{:S(2)}, u32[]{:S(2)}) collective-permute-start(bf16[4,120,640]{2,1,0:T(8,128)(2,1)S(1)} %get-tuple-element.128), channel_id=1, source_target_pairs={{0,16},{1,3},{2,18},{3,1},{4,20},{5,7},{6,22},{7,5},{8,24},{9,11},... | collective-permute-start | bytes 1843208 | tf_op jit(solution)/shard_map/ppermute | solution.py:92
  43.9 24.7 %collective-permute-start.5 = (bf16[2,4,120,640]{3,2,1,0:T(8,128)(2,1)S(1)}, bf16[2,4,120,640]{3,2,1,0:T(8,128)(2,1)S(1)}, u32[]{:S(2)}, u32[]{:S(2)}) collective-permute-start(bf16[2,4,120,640]{3,2,1,0:T(8,128)(2,1)S(1)} %get-tuple-element.112), channel_id=1, source_target_pairs={{0,2},{1,17},{2,0},{3,19},{4,6},{5,21},{6,4},{7,23},{8,10},{9,25},... | collective-permute-start | bytes 3686408 | tf_op jit(solution)/shard_map/ppermute | solution.py:92
  68.6 8.1 %copy-start.49 = (s32[1,512]{1,0:T(1,128)S(1)}, s32[1,512]{1,0:T(1,128)}, u32[]{:S(2)}) copy-start(s32[1,512]{1,0:T(1,128)} %param.12) | copy-start | bytes 6148
  68.6 8.1 %copy-start.50 = (bf16[60]{0:T(256)(128)(2,1)S(1)}, bf16[60]{0:T(256)(128)(2,1)}, u32[]{:S(2)}) copy-start(bf16[60]{0:T(256)(128)(2,1)} %param.16) | copy-start | bytes 364
  68.6 8.1 %copy-start.51 = (bf16[60]{0:T(256)(128)(2,1)S(1)}, bf16[60]{0:T(256)(128)(2,1)}, u32[]{:S(2)}) copy-start(bf16[60]{0:T(256)(128)(2,1)} %param.13) | copy-start | bytes 364
  68.6 44.9 %copy-start.5 = (bf16[512,960]{0,1:T(8,128)(2,1)S(1)}, bf16[512,960]{0,1:T(8,128)(2,1)}, u32[]{:S(2)}) copy-start(bf16[512,960]{0,1:T(8,128)(2,1)} %param.10) | copy-start | bytes 2949124
  70.5 43.7 %copy-start.48 = (s32[1,512]{1,0:T(1,128)S(1)}, s32[1,512]{1,0:T(1,128)}, u32[]{:S(2)}) copy-start(s32[1,512]{1,0:T(1,128)} %param.11) | copy-start | bytes 6148
  70.5 44.5 %collective-permute-start.6 = (bf16[2,2,4,120,640]{4,3,2,1,0:T(8,128)(2,1)}, bf16[2,2,4,120,640]{4,3,2,1,0:T(8,128)(2,1)}, u32[]{:S(2)}, u32[]{:S(2)}) collective-permute-start(bf16[2,2,4,120,640]{4,3,2,1,0:T(8,128)(2,1)} %get-tuple-element.86), channel_id=1, source_target_pairs={{0,1},{1,0},{2,3},{3,2},{4,5},{5,4},{6,7},{7,6},{8,9},{9,8},{10,11... | collective-permute-start | bytes 7372808 | tf_op jit(solution)/shard_map/ppermute | solution.py:92
  113.8 6.9 %copy-start.43 = (f32[1,960]{1,0:T(1,128)}, f32[1,960]{1,0:T(1,128)S(1)}, u32[]{:S(2)}) copy-start(f32[1,960]{1,0:T(1,128)S(1)} %get-tuple-element.138) | copy-start | bytes 11524
  114.2 12.3 %copy-start.20 = (f32[512,32]{0,1:T(8,128)}, f32[512,32]{0,1:T(8,128)S(1)}, u32[]{:S(2)}) copy-start(f32[512,32]{0,1:T(8,128)S(1)} %get-tuple-element.140) | copy-start | bytes 196612
  115.0 5.8 %copy-start.46 = (f32[512]{0:T(512)}, f32[512]{0:T(512)S(1)}, u32[]{:S(2)}) copy-start(f32[512]{0:T(512)S(1)} %get-tuple-element.142) | copy-start | bytes 6148
  119.7 31.0 %copy-start.41 = (bf16[960,64]{1,0:T(8,128)(2,1)}, bf16[960,64]{1,0:T(8,128)(2,1)S(1)}, u32[]{:S(2)}) copy-start(bf16[960,64]{1,0:T(8,128)(2,1)S(1)} %slice.208) | copy-start | bytes 368644
  120.8 29.9 %copy-start.26 = (bf16[4,2,120,640]{3,2,1,0:T(8,128)(2,1)}, bf16[4,2,120,640]{3,2,1,0:T(8,128)(2,1)S(1)}, u32[]{:S(2)}) copy-start(bf16[4,2,120,640]{3,2,1,0:T(8,128)(2,1)S(1)} %pad_maximum_fusion.11) | copy-start | bytes 3686404
  123.6 19.1 %copy-start.11 = (bf16[512,320]{0,1:T(8,128)(2,1)}, bf16[512,320]{0,1:T(8,128)(2,1)S(1)}, u32[]{:S(2)}) copy-start(bf16[512,320]{0,1:T(8,128)(2,1)S(1)} %slice.260) | copy-start | bytes 983044
  125.7 25.1 %copy-start.29 = (bf16[4,2,120,640]{3,2,1,0:T(8,128)(2,1)}, bf16[4,2,120,640]{3,2,1,0:T(8,128)(2,1)S(1)}, u32[]{:S(2)}) copy-start(bf16[4,2,120,640]{3,2,1,0:T(8,128)(2,1)S(1)} %pad_maximum_fusion.12) | copy-start | bytes 3686404
  126.5 8.4 %copy-start.34 = (bf16[512,5,32]{0,2,1:T(8,128)(2,1)}, bf16[512,5,32]{0,2,1:T(8,128)(2,1)S(1)}, u32[]{:S(2)}) copy-start(bf16[512,5,32]{0,2,1:T(8,128)(2,1)S(1)} %get-tuple-element.119) | copy-start | bytes 491524
  126.5 8.4 %copy-start.35 = (bf16[512,5,32]{0,2,1:T(8,128)(2,1)}, bf16[512,5,32]{0,2,1:T(8,128)(2,1)S(1)}, u32[]{:S(2)}) copy-start(bf16[512,5,32]{0,2,1:T(8,128)(2,1)S(1)} %get-tuple-element.120) | copy-start | bytes 491524
  127.9 7.0 %copy-start.14 = (bf16[512,15,32]{0,2,1:T(8,128)(2,1)}, bf16[512,15,32]{0,2,1:T(8,128)(2,1)S(1)}, u32[]{:S(2)}) copy-start(bf16[512,15,32]{0,2,1:T(8,128)(2,1)S(1)} %get-tuple-element.90) | copy-start | bytes 1474564
  127.9 7.0 %copy-start.16 = (bf16[512,15,32]{0,2,1:T(8,128)(2,1)}, bf16[512,15,32]{0,2,1:T(8,128)(2,1)S(1)}, u32[]{:S(2)}) copy-start(bf16[512,15,32]{0,2,1:T(8,128)(2,1)S(1)} %get-tuple-element.91) | copy-start | bytes 1474564
  152.0 52.2 %copy-start.3 = (f32[512,960]{0,1:T(8,128)}, f32[512,960]{0,1:T(8,128)S(1)}, u32[]{:S(2)}) copy-start(f32[512,960]{0,1:T(8,128)S(1)} %get-tuple-element.154) | copy-start | bytes 5898244
  152.1 20.3 %copy-start.31 = (bf16[512,960]{0,1:T(8,128)(2,1)S(1)}, bf16[512,960]{0,1:T(8,128)(2,1)}, u32[]{:S(2)}) copy-start(bf16[512,960]{0,1:T(8,128)(2,1)} %param.19) | copy-start | bytes 2949124
  182.6 26.8 %copy-start.54 = (bf16[512,2560]{1,0:T(8,128)(2,1)}, bf16[512,2560]{1,0:T(8,128)(2,1)S(1)}, u32[]{:S(2)}) copy-start(bf16[512,2560]{1,0:T(8,128)(2,1)S(1)} %get-tuple-element.55) | copy-start | bytes 7864324
  208.1 62.5 %copy-start = (f32[512,960]{0,1:T(8,128)}, f32[512,960]{0,1:T(8,128)S(1)}, u32[]{:S(2)}) copy-start(f32[512,960]{0,1:T(8,128)S(1)} %subtract_add_fusion) | copy-start | bytes 5898244
  225.9 8.7 %copy-start.12 = (bf16[512,320]{0,1:T(8,128)(2,1)S(1)}, bf16[512,320]{0,1:T(8,128)(2,1)}, u32[]{:S(2)}) copy-start(bf16[512,320]{0,1:T(8,128)(2,1)} %copy-done.11) | copy-start | bytes 983044
  225.9 67.7 %collective-permute-start.22 = (bf16[4,2,2,80,960]{4,3,0,2,1:T(8,128)(2,1)}, bf16[4,2,2,80,960]{4,3,0,2,1:T(8,128)(2,1)}, u32[]{:S(2)}, u32[]{:S(2)}) collective-permute-start(bf16[4,2,2,80,960]{4,3,0,2,1:T(8,128)(2,1)} %copy_bitcast_fusion), channel_id=1, source_target_pairs={{0,1},{1,0},{2,3},{3,2},{4,5},{5,4},{6,7},{7,6},{8,9},{9,8},{10,11... | collective-permute-start | bytes 7372808 | tf_op jit(solution)/shard_map/ppermute | solution.py:92
  234.3 51.6 %collective-permute-start.13 = (bf16[960,2560]{1,0:T(8,128)(2,1)}, bf16[960,2560]{1,0:T(8,128)(2,1)}, u32[]{:S(2)}, u32[]{:S(2)}) collective-permute-start(bf16[960,2560]{1,0:T(8,128)(2,1)} %get-tuple-element.69), channel_id=1, source_target_pairs={{0,1},{1,0},{2,3},{3,2},{4,5},{5,4},{6,7},{7,6},{8,9},{9,8},{10,11... | collective-permute-start | bytes 14745608 | tf_op jit(solution)/shard_map/ppermute | solution.py:92
  234.5 12.8 %slice-start = ((s8[15728640]{0:T(1024)(128)(4,1)}), s8[4194304]{0:T(1024)(128)(4,1)S(1)}, s32[]{:S(2)}) async-start(s8[15728640]{0:T(1024)(128)(4,1)} %bitcast.277), calls=%async_computation.2 | async-start | bytes 8388608
  234.5 12.8 %slice-start.1 = ((s8[15728640]{0:T(1024)(128)(4,1)}), s8[4194304]{0:T(1024)(128)(4,1)S(1)}, s32[]{:S(2)}) async-start(s8[15728640]{0:T(1024)(128)(4,1)} %bitcast.277), calls=%async_computation.3 | async-start | bytes 8388608
  234.5 14.6 %slice-start.2 = ((s8[15728640]{0:T(1024)(128)(4,1)}), s8[4194304]{0:T(1024)(128)(4,1)S(1)}, s32[]{:S(2)}) async-start(s8[15728640]{0:T(1024)(128)(4,1)} %bitcast.277), calls=%async_computation.4 | async-start | bytes 8388608
  234.5 15.5 %slice-start.3 = ((s8[15728640]{0:T(1024)(128)(4,1)}), s8[3145728]{0:T(1024)(128)(4,1)S(1)}, s32[]{:S(2)}) async-start(s8[15728640]{0:T(1024)(128)(4,1)} %bitcast.277), calls=%async_computation.5 | async-start | bytes 6291456
  250.0 7.7 %copy-start.15 = (bf16[512,15,32]{0,2,1:T(8,128)(2,1)S(1)}, bf16[512,15,32]{0,2,1:T(8,128)(2,1)}, u32[]{:S(2)}) copy-start(bf16[512,15,32]{0,2,1:T(8,128)(2,1)} %copy-done.14) | copy-start | bytes 1474564
  250.0 7.8 %copy-start.17 = (bf16[512,15,32]{0,2,1:T(8,128)(2,1)S(1)}, bf16[512,15,32]{0,2,1:T(8,128)(2,1)}, u32[]{:S(2)}) copy-start(bf16[512,15,32]{0,2,1:T(8,128)(2,1)} %copy-done.16) | copy-start | bytes 1474564
  260.4 6.9 %copy-start.37 = (bf16[512,5,64]{0,2,1:T(8,128)(2,1)}, bf16[512,5,64]{0,2,1:T(8,128)(2,1)S(1)}, u32[]{:S(2)}) copy-start(bf16[512,5,64]{0,2,1:T(8,128)(2,1)S(1)} %pad_maximum_fusion.23) | copy-start | bytes 983044
  282.6 20.2 %slice-start.10 = ((s8[5242880]{0:T(1024)(128)(4,1)}), s8[4194304]{0:T(1024)(128)(4,1)S(1)}, s32[]{:S(2)}) async-start(s8[5242880]{0:T(1024)(128)(4,1)} %bitcast.347), calls=%async_computation.12 | async-start | bytes 8388608
  285.5 13.7 %collective-permute-start.7 = (bf16[960,1280]{1,0:T(8,128)(2,1)S(1)}, bf16[960,1280]{1,0:T(8,128)(2,1)S(1)}, u32[]{:S(2)}, u32[]{:S(2)}) collective-permute-start(bf16[960,1280]{1,0:T(8,128)(2,1)S(1)} %get-tuple-element.75), channel_id=1, source_target_pairs={{0,1},{1,0},{2,3},{3,2},{4,5},{5,4},{6,7},{7,6},{8,9},{9,8},{10,11... | collective-permute-start | bytes 7372808 | tf_op jit(solution)/shard_map/ppermute | solution.py:92
  289.3 13.5 %slice-start.11 = ((s8[5242880]{0:T(1024)(128)(4,1)}), s8[1048576]{0:T(1024)(128)(4,1)S(1)}, s32[]{:S(2)}) async-start(s8[5242880]{0:T(1024)(128)(4,1)} %bitcast.347), calls=%async_computation.13 | async-start | bytes 2097152
  289.3 48.4 %collective-permute-start.14 = (bf16[2,4,120,1280]{3,2,1,0:T(8,128)(2,1)S(1)}, bf16[2,4,120,1280]{3,2,1,0:T(8,128)(2,1)S(1)}, u32[]{:S(2)}, u32[]{:S(2)}) collective-permute-start(bf16[2,4,120,1280]{3,2,1,0:T(8,128)(2,1)S(1)} %pad_maximum_fusion.4), channel_id=1, source_target_pairs={{0,2},{1,17},{2,0},{3,19},{4,6},{5,21},{6,4},{7,23},{8,10},{9,25},... | collective-permute-start | bytes 7372808 | tf_op jit(solution)/shard_map/ppermute | solution.py:92
  296.0 37.3 %collective-permute-start.23 = (bf16[2,4,80,960]{3,2,1,0:T(8,128)(2,1)S(1)}, bf16[2,4,80,960]{3,2,1,0:T(8,128)(2,1)S(1)}, u32[]{:S(2)}, u32[]{:S(2)}) collective-permute-start(bf16[2,4,80,960]{3,2,1,0:T(8,128)(2,1)S(1)} %pad_maximum_fusion.7), channel_id=1, source_target_pairs={{0,2},{1,17},{2,0},{3,19},{4,6},{5,21},{6,4},{7,23},{8,10},{9,25},... | collective-permute-start | bytes 3686408 | tf_op jit(solution)/shard_map/ppermute | solution.py:92
  302.1 96.6 %collective-permute-start.8 = (bf16[2,4,120,640]{3,2,1,0:T(8,128)(2,1)}, bf16[2,4,120,640]{3,2,1,0:T(8,128)(2,1)}, u32[]{:S(2)}, u32[]{:S(2)}) collective-permute-start(bf16[2,4,120,640]{3,2,1,0:T(8,128)(2,1)} %pad_maximum_fusion.13), channel_id=1, source_target_pairs={{0,2},{1,17},{2,0},{3,19},{4,6},{5,21},{6,4},{7,23},{8,10},{9,25},... | collective-permute-start | bytes 3686408 | tf_op jit(solution)/shard_map/ppermute | solution.py:92
  333.3 8.6 %copy-start.22 = (bf16[2,4,80,960]{3,2,1,0:T(8,128)(2,1)}, bf16[2,4,80,960]{3,2,1,0:T(8,128)(2,1)S(1)}, u32[]{:S(2)}) copy-start(bf16[2,4,80,960]{3,2,1,0:T(8,128)(2,1)S(1)} %collective-permute-done.23) | copy-start | bytes 3686404
  336.2 67.1 %collective-permute-start.24 = (bf16[4,80,960]{2,1,0:T(8,128)(2,1)}, bf16[4,80,960]{2,1,0:T(8,128)(2,1)S(1)}, u32[]{:S(2)}, u32[]{:S(2)}) collective-permute-start(bf16[4,80,960]{2,1,0:T(8,128)(2,1)} %fusion.40), channel_id=1, source_target_pairs={{0,16},{1,3},{2,18},{3,1},{4,20},{5,7},{6,22},{7,5},{8,24},{9,11},... | collective-permute-start | bytes 1843208 | tf_op jit(solution)/shard_map/ppermute | solution.py:92
  341.8 72.2 %collective-permute-start.15 = (bf16[4,120,1280]{2,1,0:T(8,128)(2,1)}, bf16[4,120,1280]{2,1,0:T(8,128)(2,1)}, u32[]{:S(2)}, u32[]{:S(2)}) collective-permute-start(bf16[4,120,1280]{2,1,0:T(8,128)(2,1)} %fusion.21), channel_id=1, source_target_pairs={{0,16},{1,3},{2,18},{3,1},{4,20},{5,7},{6,22},{7,5},{8,24},{9,11},... | collective-permute-start | bytes 3686408 | tf_op jit(solution)/shard_map/ppermute | solution.py:92
  398.7 4.6 copy-start.23
  400.3 10.5 %collective-permute-start.9 = (bf16[4,120,640]{2,1,0:T(8,128)(2,1)S(1)}, bf16[4,120,640]{2,1,0:T(8,128)(2,1)S(1)}, u32[]{:S(2)}, u32[]{:S(2)}) collective-permute-start(bf16[4,120,640]{2,1,0:T(8,128)(2,1)S(1)} %fusion.52), channel_id=1, source_target_pairs={{0,16},{1,3},{2,18},{3,1},{4,20},{5,7},{6,22},{7,5},{8,24},{9,11},... | collective-permute-start | bytes 1843208 | tf_op jit(solution)/shard_map/ppermute | solution.py:92
  405.1 14.2 %collective-permute-start.25 = (bf16[80,960]{1,0:T(8,128)(2,1)S(1)}, bf16[80,960]{1,0:T(8,128)(2,1)S(1)}, u32[]{:S(2)}, u32[]{:S(2)}) collective-permute-start(bf16[80,960]{1,0:T(8,128)(2,1)S(1)} %get-tuple-element.121), channel_id=1, source_target_pairs={{0,4},{1,5},{2,6},{3,7},{4,8},{5,9},{6,10},{7,11},{8,12},{9,13},{1... | collective-permute-start | bytes 460808 | tf_op jit(solution)/shard_map/ppermute | solution.py:92
  406.7 15.5 %collective-permute-start.27 = (bf16[80,960]{1,0:T(8,128)(2,1)S(1)}, bf16[80,960]{1,0:T(8,128)(2,1)S(1)}, u32[]{:S(2)}, u32[]{:S(2)}) collective-permute-start(bf16[80,960]{1,0:T(8,128)(2,1)S(1)} %get-tuple-element.122), channel_id=1, source_target_pairs={{0,12},{1,13},{2,14},{3,15},{4,0},{5,1},{6,2},{7,3},{8,4},{9,5},{1... | collective-permute-start | bytes 460808 | tf_op jit(solution)/shard_map/ppermute | solution.py:92
  409.0 7.6 %copy-start.10 = (bf16[2,4,120,1280]{3,2,1,0:T(8,128)(2,1)S(1)}, bf16[2,4,120,1280]{3,2,1,0:T(8,128)(2,1)}, u32[]{:S(2)}) copy-start(bf16[2,4,120,1280]{3,2,1,0:T(8,128)(2,1)} %copy-done.9) | copy-start | bytes 7372804
  409.0 25.7 %collective-permute-start.26 = (bf16[80,960]{1,0:T(8,128)(2,1)S(1)}, bf16[80,960]{1,0:T(8,128)(2,1)S(1)}, u32[]{:S(2)}, u32[]{:S(2)}) collective-permute-start(bf16[80,960]{1,0:T(8,128)(2,1)S(1)} %get-tuple-element.123), channel_id=1, source_target_pairs={{0,8},{1,9},{2,10},{3,11},{4,12},{5,13},{6,14},{7,15},{8,0},{9,1},... | collective-permute-start | bytes 460808 | tf_op jit(solution)/shard_map/ppermute | solution.py:92
  412.5 22.2 %collective-permute-start.10 = (bf16[120,640]{1,0:T(8,128)(2,1)S(1)}, bf16[120,640]{1,0:T(8,128)(2,1)S(1)}, u32[]{:S(2)}, u32[]{:S(2)}) collective-permute-start(bf16[120,640]{1,0:T(8,128)(2,1)S(1)} %get-tuple-element.124), channel_id=1, source_target_pairs={{0,4},{1,5},{2,6},{3,7},{4,8},{5,9},{6,10},{7,11},{8,12},{9,13},{1... | collective-permute-start | bytes 460808 | tf_op jit(solution)/shard_map/ppermute | solution.py:92
  414.1 21.8 %collective-permute-start.12 = (bf16[120,640]{1,0:T(8,128)(2,1)S(1)}, bf16[120,640]{1,0:T(8,128)(2,1)S(1)}, u32[]{:S(2)}, u32[]{:S(2)}) collective-permute-start(bf16[120,640]{1,0:T(8,128)(2,1)S(1)} %get-tuple-element.125), channel_id=1, source_target_pairs={{0,12},{1,13},{2,14},{3,15},{4,0},{5,1},{6,2},{7,3},{8,4},{9,5},{1... | collective-permute-start | bytes 460808 | tf_op jit(solution)/shard_map/ppermute | solution.py:92
  419.3 30.0 %collective-permute-start.11 = (bf16[120,640]{1,0:T(8,128)(2,1)S(1)}, bf16[120,640]{1,0:T(8,128)(2,1)S(1)}, u32[]{:S(2)}, u32[]{:S(2)}) collective-permute-start(bf16[120,640]{1,0:T(8,128)(2,1)S(1)} %get-tuple-element.126), channel_id=1, source_target_pairs={{0,8},{1,9},{2,10},{3,11},{4,12},{5,13},{6,14},{7,15},{8,0},{9,1},... | collective-permute-start | bytes 460808 | tf_op jit(solution)/shard_map/ppermute | solution.py:92
  422.2 27.3 %collective-permute-start.16 = (bf16[120,1280]{1,0:T(8,128)(2,1)S(1)}, bf16[120,1280]{1,0:T(8,128)(2,1)S(1)}, u32[]{:S(2)}, u32[]{:S(2)}) collective-permute-start(bf16[120,1280]{1,0:T(8,128)(2,1)S(1)} %get-tuple-element.92), channel_id=1, source_target_pairs={{0,4},{1,5},{2,6},{3,7},{4,8},{5,9},{6,10},{7,11},{8,12},{9,13},{1... | collective-permute-start | bytes 921608 | tf_op jit(solution)/shard_map/ppermute | solution.py:92
  434.7 14.7 %collective-permute-start.18 = (bf16[120,1280]{1,0:T(8,128)(2,1)S(1)}, bf16[120,1280]{1,0:T(8,128)(2,1)S(1)}, u32[]{:S(2)}, u32[]{:S(2)}) collective-permute-start(bf16[120,1280]{1,0:T(8,128)(2,1)S(1)} %get-tuple-element.93), channel_id=1, source_target_pairs={{0,12},{1,13},{2,14},{3,15},{4,0},{5,1},{6,2},{7,3},{8,4},{9,5},{1... | collective-permute-start | bytes 921608 | tf_op jit(solution)/shard_map/ppermute | solution.py:92
  434.7 26.1 %collective-permute-start.17 = (bf16[120,1280]{1,0:T(8,128)(2,1)S(1)}, bf16[120,1280]{1,0:T(8,128)(2,1)S(1)}, u32[]{:S(2)}, u32[]{:S(2)}) collective-permute-start(bf16[120,1280]{1,0:T(8,128)(2,1)S(1)} %get-tuple-element.94), channel_id=1, source_target_pairs={{0,8},{1,9},{2,10},{3,11},{4,12},{5,13},{6,14},{7,15},{8,0},{9,1},... | collective-permute-start | bytes 921608 | tf_op jit(solution)/shard_map/ppermute | solution.py:92
  435.9 27.5 %collective-permute-start.28 = (bf16[80,960]{1,0:T(8,128)(2,1)S(1)}, bf16[80,960]{1,0:T(8,128)(2,1)S(1)}, u32[]{:S(2)}, u32[]{:S(2)}) collective-permute-start(bf16[80,960]{1,0:T(8,128)(2,1)S(1)} %fusion.73), channel_id=1, source_target_pairs={{0,16},{1,17},{2,18},{3,19},{4,20},{5,21},{6,22},{7,23},{8,24},{9,... | collective-permute-start | bytes 460808 | tf_op jit(solution)/shard_map/ppermute | solution.py:92
  461.2 13.7 %collective-permute-start.20 = (bf16[60,1920]{1,0:T(8,128)(2,1)S(1)}, bf16[60,1920]{1,0:T(8,128)(2,1)S(1)}, u32[]{:S(2)}, u32[]{:S(2)}) collective-permute-start(bf16[60,1920]{1,0:T(8,128)(2,1)S(1)} %get-tuple-element.130), channel_id=1, source_target_pairs={{0,1},{1,0},{2,3},{3,2},{4,5},{5,4},{6,7},{7,6},{8,9},{9,8},{10,11... | collective-permute-start | bytes 691208 | tf_op jit(solution)/shard_map/ppermute | solution.py:92
  461.3 13.6 %collective-permute-start.21 = (bf16[60,1920]{1,0:T(8,128)(2,1)S(1)}, bf16[60,1920]{1,0:T(8,128)(2,1)S(1)}, u32[]{:S(2)}, u32[]{:S(2)}) collective-permute-start(bf16[60,1920]{1,0:T(8,128)(2,1)S(1)} %get-tuple-element.130), channel_id=1, source_target_pairs={{0,17},{1,16},{2,19},{3,18},{4,21},{5,20},{6,23},{7,22},{8,25},{9,... | collective-permute-start | bytes 691208 | tf_op jit(solution)/shard_map/ppermute | solution.py:92
  462.9 11.9 %collective-permute-start.19 = (bf16[60,1920]{1,0:T(8,128)(2,1)S(1)}, bf16[60,1920]{1,0:T(8,128)(2,1)S(1)}, u32[]{:S(2)}, u32[]{:S(2)}) collective-permute-start(bf16[60,1920]{1,0:T(8,128)(2,1)S(1)} %get-tuple-element.129), channel_id=1, source_target_pairs={{0,16},{1,17},{2,18},{3,19},{4,20},{5,21},{6,22},{7,23},{8,24},{9,... | collective-permute-start | bytes 691208 | tf_op jit(solution)/shard_map/ppermute | solution.py:92
  (35 other events, 81.6 us)
Sparse Core Ops, SparseCore 0:
  10.9 101.4 all-gather.3
  114.7 57.6 all-gather.5

commit v2 on v0

v2 whole, which is shorter than its diff:
```python
import functools

import jax
import jax.numpy as jnp
from jax import lax
from jax.experimental import pallas as pl
from jax.experimental.pallas import tpu as pltpu
from jax.sharding import PartitionSpec as P

HEADS = 15
KV_HEADS = 5
HD = 64
GROUP = HEADS // KV_HEADS

EPSILON = 1e-05
ROPE_BASE = 100000.0
NEG_FILL = -1e30

AXES = ("rep", "shard")
F32 = jnp.float32
BF16 = jnp.bfloat16
LANES = 128
MIB = 1024 * 1024


def hop(values, shards, move):
    pairs = []
    for rep in range(2):
        for outer in range(shards // 4):
            for mid in range(2):
                for core in range(2):
                    to = move(rep, outer, mid, core)
                    pairs.append(
                        (
                            rep * shards + outer * 4 + mid * 2 + core,
                            to[0] * shards + to[1] * 4 + to[2] * 2 + to[3],
                        )
                    )
    return lax.ppermute(values, AXES, pairs)


def core_move(rep, outer, mid, core):
    return (rep, outer, mid, 1 - core)


def rep_move(rep, outer, mid, core):
    return (1 - rep, outer, mid, core)


def cross_move(rep, outer, mid, core):
    return (1 - rep, outer, mid, 1 - core)


def first_move(rep, outer, mid, core):
    return (rep, outer, 1 - mid, core) if core == 0 else (1 - rep, outer, mid, core)


def second_move(rep, outer, mid, core):
    return (1 - rep, outer, mid, core) if core == 0 else (rep, outer, 1 - mid, core)


def outer_move(step, count):
    return lambda rep, outer, mid, core: (rep, (outer + step) % count, mid, core)


class Order:
    def __init__(self):
        self.done = None

    def after(self, *values):
        if self.done is not None:
            values = lax.optimization_barrier(tuple(values) + (self.done,))[:-1]
        return values if len(values) > 1 else values[0]

    def mark(self, value):
        self.done = value
        return value


def pick(array, index):
    return lax.dynamic_index_in_dim(array, index, 0, keepdims=False)


def place():
    shard = lax.axis_index("shard")
    return lax.axis_index("rep"), shard // 4, (shard // 2) % 2, shard % 2


def settle_kernel(by_rows, where_ref, held_ref, came_ref, out_ref, sem):
    rep, mid, core = where_ref[0], where_ref[2], where_ref[3]
    for second, source in enumerate((held_ref, came_ref)):
        for first in range(2):
            to_mid = jnp.where(core == 0, mid ^ second, mid ^ first)
            to_rep = jnp.where(core == 0, rep ^ first, rep ^ second)
            for step in range(held_ref.shape[1]):
                to = out_ref.at[step, to_mid, to_rep] if by_rows else out_ref.at[to_rep, step, to_mid]
                pltpu.make_async_copy(source.at[first, step], to, sem).start()
    for source in (held_ref, came_ref):
        pltpu.make_async_copy(source, source, sem).wait()


def settle(held, came, where, by_rows):
    _, count, rows, width = held.shape
    shape = (count, 2, 2) if by_rows else (2, count, 2)
    any_space = pl.BlockSpec(memory_space=pl.ANY)
    out = pl.pallas_call(
        functools.partial(settle_kernel, by_rows),
        out_shape=jax.ShapeDtypeStruct(shape + (rows, width), held.dtype),
        in_specs=[pl.BlockSpec(memory_space=pltpu.SMEM), any_space, any_space],
        out_specs=pl.BlockSpec(memory_space=pltpu.VMEM),
        scratch_shapes=[pltpu.SemaphoreType.DMA],
        compiler_params=pltpu.CompilerParams(vmem_limit_bytes=8 * MIB),
        cost_estimate=SHORT,
        name="settle",
    )(where, held, came)
    return out.reshape(shape[:2] + (2 * rows, width))


def roll_steps(array, axis):
    count = array.shape[axis]
    outer = place()[1]
    parts = [
        lax.dynamic_index_in_dim(array, (outer - k) % count, axis, keepdims=True)
        for k in range(count)
    ]
    return jnp.concatenate(parts, axis)


def assemble_kernel(where_ref, own_ref, came_ref, out_ref, sem):
    outer, core = where_ref[1], where_ref[3]
    _, count, rows, width = own_ref.shape
    for source, half in ((own_ref, core), (came_ref, 1 - core)):
        for rep in range(2):
            column = pl.multiple_of((half * 2 + rep) * width, LANES)
            for step in range(count):
                row = pl.multiple_of(lax.rem(outer + count - step, count) * rows, 16)
                pltpu.make_async_copy(
                    source.at[rep, step],
                    out_ref.at[pl.ds(row, rows), pl.ds(column, width)],
                    sem,
                ).start()
    pltpu.make_async_copy(out_ref, out_ref, sem).wait()


def assemble(own, came, where):
    _, count, rows, width = own.shape
    core = where[3]
    shape = (count * rows, 4 * width)
    if rows % 16 or width % LANES:
        halves = roll_steps(jnp.stack([own, came]), 2)
        halves = jnp.stack([pick(halves, core), pick(halves, 1 - core)])
        return halves.transpose(2, 3, 0, 1, 4).reshape(shape)
    return pl.pallas_call(
        assemble_kernel,
        out_shape=jax.ShapeDtypeStruct(shape, own.dtype),
        in_specs=[
            pl.BlockSpec(memory_space=pltpu.SMEM),
            pl.BlockSpec(memory_space=pl.ANY),
            pl.BlockSpec(memory_space=pl.ANY),
        ],
        out_specs=pl.BlockSpec(memory_space=pltpu.VMEM),
        scratch_shapes=[pltpu.SemaphoreType.DMA],
        compiler_params=pltpu.CompilerParams(vmem_limit_bytes=16 * MIB),
        cost_estimate=LONG,
        name="assemble",
    )(where, own, came)


def add_low(*terms):
    total = terms[0].astype(F32)
    for term in terms[1:]:
        total = total + term.astype(F32)
    return total.astype(BF16)


class Reduction:
    def __init__(self, terms, piece, shards):
        self.terms, self.piece, self.shards = terms, piece, shards

    def parts(self, where):
        return [self.piece(term, *where) for term in self.terms]

    def first(self, order, *way):
        rep, _, mid, core = place()
        got = order.after(*self.terms, *way)
        self.terms = got if isinstance(got, tuple) else (got,)
        away = [(1 - mid, 0), (1 - mid, 1)], [(0, 1 - rep), (1, 1 - rep)]
        sums = []
        for k in range(2):
            where = tuple(jnp.where(core == 0, away[0][k][d], away[1][k][d]) for d in range(2))
            sums.append(add_low(*self.parts(where)))
        self.way = hop(order.mark(jnp.stack(sums)), self.shards, first_move)

    def second(self, order):
        rep, _, mid, core = place()
        self.got = order.after(self.way)
        self.last = jnp.where(core == 0, rep, mid)
        k = 1 - self.last
        where = jnp.where(core == 0, mid, k), jnp.where(core == 0, k, rep)
        out = order.mark(add_low(*self.parts(where), pick(self.got, k)))
        self.way = hop(out, self.shards, second_move)

    def third(self, order):
        rep, _, mid, _ = place()
        came = order.after(self.way)
        return order.mark(add_low(*self.parts((mid, rep)), pick(self.got, self.last), came))


def send_outer(mine, shards):
    outer = place()[1]
    count = shards // 4
    return [pick(mine, outer)] + [
        hop(pick(mine, (outer + k) % count), shards, outer_move(k, count)) for k in range(1, count)
    ]


def send_down(mine, shards):
    rep, outer, mid, core = place()
    count = shards // 4
    half = count // 2

    def move(step):
        pairs = []
        for r in range(2):
            for o in range(count):
                for m in range(2):
                    for c in range(2):
                        to = (o + step) % count
                        if to // half == c:
                            base = r * shards + m * 2 + c
                            pairs.append((base + o * 4, base + to * 4))
        return pairs

    return [pick(mine, outer % half)] + [
        lax.ppermute(pick(mine, (outer + k) % count % half), AXES, move(k))
        for k in range(1, count)
    ]


def share_down(total, shards):
    rep, outer, mid, core = place()
    came = hop(pick(total, 1 - core), shards, core_move)
    mine = jnp.where(outer // (shards // 8) == core, pick(total, core), came)
    stack = jnp.stack([mine, hop(mine, shards, rep_move)])
    return jnp.concatenate([pick(stack, rep), pick(stack, 1 - rep)], 0)


def share_columns(total, shards):
    rep, _, _, core = place()
    rows = total.shape[0] // 2
    halves = total.reshape(2, rows, total.shape[1])
    mine, other = pick(halves, core), pick(halves, 1 - core)
    stack = jnp.stack(
        [
            mine,
            hop(mine, shards, rep_move),
            hop(other, shards, core_move),
            hop(other, shards, cross_move),
        ]
    )
    return [pick(stack, q ^ (core * 2 + rep)) for q in range(4)]


LONG = pl.CostEstimate(flops=200 * 10**9, bytes_accessed=0, transcendentals=0)
SHORT = pl.CostEstimate(flops=10**6, bytes_accessed=0, transcendentals=0)


def dot(left, right, left_dim, right_dim):
    return lax.dot_general(
        left, right, (((left_dim,), (right_dim,)), ((), ())), preferred_element_type=F32
    )


def project_kernel(normed_ref, weight_ref, cos_ref, sin_ref, out_ref):
    half = HD // 2
    turned = (HEADS + KV_HEADS) * HD
    cosine, sine = cos_ref[...], sin_ref[...]
    normed = normed_ref[...]
    for start in range(0, turned, 2 * LANES):
        raw = dot(weight_ref[:, start : start + 2 * LANES], normed, 0, 0)
        for at in range(0, 2 * LANES, HD):
            row = start + at
            scale = 0.125 if row < HEADS * HD else 1.0
            upper, lower = raw[at : at + half], raw[at + half : at + HD]
            out_ref[row : row + half] = ((upper * cosine - lower * sine) * scale).astype(BF16)
            out_ref[row + half : row + HD] = ((lower * cosine + upper * sine) * scale).astype(BF16)
    out_ref[turned:] = dot(
        weight_ref[:, turned : turned + KV_HEADS * HD], normed, 0, 0
    ).astype(BF16)


def project(normed_t, weight, cosine, sine):
    return pl.pallas_call(
        project_kernel,
        out_shape=jax.ShapeDtypeStruct(((HEADS + 2 * KV_HEADS) * HD, normed_t.shape[1]), BF16),
        compiler_params=pltpu.CompilerParams(vmem_limit_bytes=24 * MIB),
        cost_estimate=SHORT,
        name="project",
    )(normed_t, weight, cosine, sine)


def split_tokens(tokens):
    block = 256 if tokens % 256 == 0 else tokens
    return [(start, start + block) for start in range(0, tokens, block)]


def attend_kernel(seg_row_ref, seg_col_ref, q_ref, k_ref, v_ref, prob_ref, mixed_ref, bias_ref):
    tokens = q_ref.shape[1]

    @pl.when(pl.program_id(0) == 0)
    def _():
        keys = lax.broadcasted_iota(jnp.int32, (tokens, tokens), 0)
        queries = lax.broadcasted_iota(jnp.int32, (tokens, tokens), 1)
        allowed = (seg_col_ref[...] == seg_row_ref[...]) & (keys <= queries)
        bias_ref[...] = jnp.where(allowed, 0.0, NEG_FILL)

    for head in range(GROUP):
        rows = slice(head * HD, (head + 1) * HD)
        for start, stop in split_tokens(tokens):
            scores = dot(k_ref[:, :stop], q_ref[rows, start:stop], 0, 0)
            scores = scores + bias_ref[:stop, start:stop]
            expo = jnp.exp(scores - jnp.max(scores, 0, keepdims=True))
            prob = (expo * (1.0 / jnp.sum(expo, 0, keepdims=True))).astype(BF16)
            prob_ref[head, :stop, start:stop] = prob
            mixed_ref[rows, start:stop] = dot(v_ref[:, :stop], prob, 1, 0).astype(BF16)


def attend(qkv, seg_row):
    tokens = qkv.shape[1]
    return pl.pallas_call(
        attend_kernel,
        grid=(KV_HEADS,),
        out_shape=(
            jax.ShapeDtypeStruct((HEADS, tokens, tokens), BF16),
            jax.ShapeDtypeStruct((HEADS * HD, tokens), BF16),
        ),
        in_specs=[
            pl.BlockSpec((1, tokens), lambda i: (0, 0)),
            pl.BlockSpec((tokens, 1), lambda i: (0, 0)),
            pl.BlockSpec((GROUP * HD, tokens), lambda i: (i, 0)),
            pl.BlockSpec((HD, tokens), lambda i: (HEADS + i, 0)),
            pl.BlockSpec((HD, tokens), lambda i: (HEADS + KV_HEADS + i, 0)),
        ],
        out_specs=(
            pl.BlockSpec((GROUP, tokens, tokens), lambda i: (i, 0, 0)),
            pl.BlockSpec((GROUP * HD, tokens), lambda i: (i, 0)),
        ),
        scratch_shapes=[pltpu.VMEM((tokens, tokens), F32)],
        compiler_params=pltpu.CompilerParams(vmem_limit_bytes=32 * MIB),
        cost_estimate=LONG,
        name="attend",
    )(seg_row.reshape(1, tokens), seg_row.reshape(tokens, 1), qkv, qkv, qkv)


def out_columns(width):
    kept = (HEADS + 2 * KV_HEADS) * HD
    tail = -kept % LANES
    return kept + tail - LANES, LANES - tail, kept + tail


def branch_kernel(mixed_ref, weight_ref, tokens_ref, after_ref, scale_ref, normed_ref):
    mixed = mixed_ref[...]
    tile, skip, rest = out_columns(weight_ref.shape[1])
    wide = weight_ref.shape[1] - rest
    last = dot(weight_ref[:, tile : tile + LANES], mixed, 0, 0)
    after_ref[:wide] = tokens_ref[:wide].astype(F32) + dot(weight_ref[:, rest:], mixed, 0, 0)
    after_ref[wide:] = tokens_ref[wide:].astype(F32) + last[skip:]
    after = after_ref[...]
    scale = lax.rsqrt(jnp.mean(after * after, 0, keepdims=True) + EPSILON)
    scale_ref[...] = scale
    normed_ref[...] = (after * scale).astype(BF16)


def branch(mixed, weight, tokens):
    width, count = tokens.shape
    return pl.pallas_call(
        branch_kernel,
        out_shape=(
            jax.ShapeDtypeStruct((width, count), F32),
            jax.ShapeDtypeStruct((1, count), F32),
            jax.ShapeDtypeStruct((width, count), BF16),
        ),
        compiler_params=pltpu.CompilerParams(vmem_limit_bytes=24 * MIB),
        cost_estimate=LONG,
        name="branch",
    )(mixed, weight, tokens)


def feed_kernel(
    ordered,
    offset,
    where_ref,
    normed_refs,
    cot_refs,
    pieces_ref,
    down_refs,
    down_grad_in_ref,
    sum_refs,
    back_refs,
    grad_ref,
    down_grad_ref,
    normed,
    cot,
    weight,
    down_all,
    down,
    inner,
    pull,
    grad,
    down_grad,
    results,
    results_low,
    sems,
    out_sems,
):
    outer, core = where_ref[1], where_ref[3]
    tokens = normed_refs[0].shape[1]
    units = down.shape[0]
    size = units // 2
    quarter = down_all.shape[0] // 2

    def load(index, copies):
        for source, to in copies:
            pltpu.make_async_copy(source, to, sems.at[index]).start()

    def ready(index, ref):
        pltpu.make_async_copy(ref, ref, sems.at[index]).wait()

    load(0, [(normed_refs[k], normed.at[:, pl.ds(k * tokens, tokens)]) for k in range(2)])
    if ordered:
        steps, rows = 1, pieces_ref.shape[2]
    else:
        steps, rows = pieces_ref.shape[1:3]
    for kind in range(2):
        load(
            1 + kind,
            [
                (
                    pieces_ref.at[rep, step, :, pl.ds(kind * size, size)],
                    weight.at[
                        pl.ds(pl.multiple_of(lax.rem(outer + steps - step, steps) * rows, 16), rows)
                        if steps > 1
                        else pl.ds(0, rows),
                        pl.ds(kind * units + rep * size, size),
                    ],
                )
                for rep in range(2)
                for step in range(steps)
            ],
        )
    load(3, [(cot_refs[k], cot.at[:, pl.ds(k * tokens, tokens)]) for k in range(2)])
    if ordered:
        load(4, [(down_refs[0], down_all)])
    else:
        half = steps // 2
        block = down_refs[0].shape[2]
        for source, owner in ((down_refs[0], core), (down_refs[1], 1 - core)):
            for at in range(half):
                step = lax.rem(outer + steps - (core * half + at), steps)
                for mid in range(2):
                    row = pl.multiple_of(((at * 2 + mid) * 2 + owner) * block, 16)
                    load(4, [(source.at[step, mid], down_all.at[pl.ds(row, block)])])
    ready(0, normed)
    ready(1, weight.at[:, pl.ds(0, units)])
    tile = 2 * LANES if units % (2 * LANES) == 0 else LANES
    for start in range(0, units, tile):
        at = pl.ds(start, tile)
        gate = dot(weight[:, at], normed[...], 0, 0)
        if start == 0:
            ready(2, weight.at[:, pl.ds(units, units)])
        up = dot(weight[:, pl.ds(units + start, tile)], normed[...], 0, 0)
        if start == 0:
            ready(3, cot)
            ready(4, down_all)
            down[:size] = down_all[offset : offset + size]
            down[size:] = down_all[quarter + offset : quarter + offset + size]
        inner_grad = dot(down[at], cot[...], 1, 0)
        sigma = 1.0 / (1.0 + jnp.exp(-gate))
        activ = gate * sigma
        inner[at] = (activ * up).astype(BF16)
        pull[at] = (inner_grad * up * (sigma + activ * (1.0 - sigma))).astype(BF16)
        pull[pl.ds(units + start, tile)] = (inner_grad * activ).astype(BF16)
        down_grad[at] = dot(inner[at], cot[...], 1, 1).astype(BF16)
    for rep in range(2):
        pltpu.make_async_copy(
            down_grad.at[pl.ds(rep * size, size)],
            down_grad_ref.at[rep, pl.ds(offset, size)],
            out_sems.at[0],
        ).start()
    for kind in range(2):
        for start in range(0, units, tile):
            at = pl.ds(kind * units + start, tile)
            grad[:, at] = dot(normed[...], pull[at], 1, 1).astype(BF16)
        for rep in range(2):
            pltpu.make_async_copy(
                grad.at[:, pl.ds(kind * units + rep * size, size)],
                grad_ref.at[rep, :, pl.ds(kind * size, size)],
                out_sems.at[1],
            ).start()
    for index, (out_refs, left, right, dim) in enumerate(
        ((back_refs, weight, pull, 1), (sum_refs, down, inner, 0))
    ):
        low = dot(left[...], right[:, pl.ds(tokens, tokens)], dim, 0)
        results_low[index] = low.astype(BF16)
        pltpu.make_async_copy(results_low.at[index], out_refs[1], out_sems.at[2 + index]).start()
        results[index] = dot(left[...], right[:, pl.ds(0, tokens)], dim, 0)
        pltpu.make_async_copy(results.at[index], out_refs[0], out_sems.at[4 + index]).start()
    pltpu.make_async_copy(down_grad, down_grad, out_sems.at[0]).wait()
    pltpu.make_async_copy(grad, grad, out_sems.at[1]).wait()
    for index in range(2):
        pltpu.make_async_copy(
            results_low.at[index], results_low.at[index], out_sems.at[2 + index]
        ).wait()
        pltpu.make_async_copy(results.at[index], results.at[index], out_sems.at[4 + index]).wait()


def feed(where, offset, normed, cot, pieces, down, down_grad):
    width, tokens = normed[0].shape
    size = pieces.shape[-1] // 2
    units = 2 * size
    count, _, block = down[0].shape[:3]
    half_units = count * 2 * block
    ordered = pieces.shape[2] % 16 != 0 or block % 16 != 0
    if ordered:
        pieces = roll_steps(pieces, 1).reshape(2, 1, width, units)
        core = where[3]
        rows = roll_steps(jnp.stack(down), 1)
        rows = jnp.stack([pick(rows, core), pick(rows, 1 - core)], 2)
        rows = rows.reshape(2, half_units, width)
        down = (pick(rows, core),)
    first_call = down_grad is None
    operands = [*normed, *cot, pieces, *down] + ([] if first_call else [down_grad])
    split = len(down)

    def body(where_ref, *refs):
        refs = list(refs)
        take = lambda count: [refs.pop(0) for _ in range(count)]
        ins = take(2), take(2), take(1)[0], take(split)
        down_grad_in = None if first_call else take(1)[0]
        feed_kernel(
            ordered, offset, where_ref, *ins, down_grad_in, take(2), take(2), *refs
        )

    wide = jax.ShapeDtypeStruct((width, tokens), F32)
    low = jax.ShapeDtypeStruct((width, tokens), BF16)
    out_shape = (
        wide,
        low,
        wide,
        low,
        jax.ShapeDtypeStruct((2, width, units), BF16),
        jax.ShapeDtypeStruct((2, half_units // 2, width), BF16),
    )
    any_space = pl.BlockSpec(memory_space=pl.ANY)
    return pl.pallas_call(
        body,
        in_specs=[pl.BlockSpec(memory_space=pltpu.SMEM)] + [any_space] * len(operands),
        out_specs=(any_space,) * len(out_shape),
        out_shape=out_shape,
        scratch_shapes=[
            pltpu.VMEM((width, 2 * tokens), BF16),
            pltpu.VMEM((width, 2 * tokens), BF16),
            pltpu.VMEM((width, 2 * units), BF16),
            pltpu.VMEM((half_units, width), BF16),
            pltpu.VMEM((units, width), BF16),
            pltpu.VMEM((units, 2 * tokens), BF16),
            pltpu.VMEM((2 * units, 2 * tokens), BF16),
            pltpu.VMEM((width, 2 * units), BF16),
            pltpu.VMEM((units, width), BF16),
            pltpu.VMEM((2, width, tokens), F32),
            pltpu.VMEM((2, width, tokens), BF16),
            pltpu.SemaphoreType.DMA((6,)),
            pltpu.SemaphoreType.DMA((6,)),
        ],
        input_output_aliases={} if first_call else {len(operands): 5},
        compiler_params=pltpu.CompilerParams(vmem_limit_bytes=52 * MIB),
        cost_estimate=LONG,
        name="feed",
    )(where, *operands)


def return_kernel(
    back_refs, after_ref, scale_ref, cot_ref, mixed_ref, weight_ref, grad_ref, mixed_grad_ref, out_grad_ref
):
    back = back_refs[0][...]
    for ref in back_refs[1:]:
        back = back + ref[...].astype(F32)
    after, scale = after_ref[...], scale_ref[...]
    mean = jnp.mean(back * after, 0, keepdims=True)
    grad = cot_ref[...].astype(F32) + scale * back - after * (scale * scale * scale * mean)
    grad_ref[...] = grad
    low = grad.astype(BF16)
    tile, skip, rest = out_columns(weight_ref.shape[1])
    wide = weight_ref.shape[1] - rest
    last = low[wide:]
    mixed_grad_ref[...] = (
        dot(weight_ref[:, rest:], low[:wide], 1, 0)
        + dot(weight_ref[:, tile + skip : rest], last, 1, 0)
    ).astype(BF16)
    mixed = mixed_ref[...]
    out_grad_ref[:, : LANES - skip] = dot(mixed, last, 1, 1).astype(BF16)
    out_grad_ref[:, LANES - skip :] = dot(mixed, low[:wide], 1, 1).astype(BF16)


def return_branch(backs, after, scale, cot, mixed, weight):
    width, count = after.shape

    def body(*refs):
        return_kernel(refs[: len(backs)], *refs[len(backs) :])

    return pl.pallas_call(
        body,
        out_shape=(
            jax.ShapeDtypeStruct((width, count), F32),
            jax.ShapeDtypeStruct((width, count), BF16),
            jax.ShapeDtypeStruct((width, width), BF16),
        ),
        compiler_params=pltpu.CompilerParams(vmem_limit_bytes=32 * MIB),
        cost_estimate=LONG,
        name="return_branch",
    )(*backs, after, scale, cot, mixed, weight)


def attend_back_kernel(
    prob_ref, mixed_ref, grad_ref, q_ref, k_ref, v_ref, cos_ref, sin_ref, dq_ref, dk_ref, dv_ref
):
    half = HD // 2
    tokens = q_ref.shape[1]
    cosine, sine = cos_ref[...], sin_ref[...]
    key_grad = [None] * len(split_tokens(tokens))
    value_grad = [None] * len(split_tokens(tokens))

    def unturn(to_ref, row, grads, columns):
        upper, lower = grads[:half], grads[half:]
        c, s = cosine[:, columns], sine[:, columns]
        to_ref[row : row + half, columns] = (upper * c + lower * s).astype(BF16)
        to_ref[row + half : row + HD, columns] = (lower * c - upper * s).astype(BF16)

    for head in range(GROUP):
        rows = slice(head * HD, (head + 1) * HD)
        for block, (start, stop) in enumerate(split_tokens(tokens)):
            grad = grad_ref[rows, start:stop]
            mixed = mixed_ref[rows, start:stop]
            row_dot = jnp.sum(grad.astype(F32) * mixed.astype(F32), 0, keepdims=True)
            prob = prob_ref[head, :stop, start:stop]
            prob_grad = dot(v_ref[:, :stop], grad, 0, 0)
            score_grad = (prob.astype(F32) * (prob_grad - row_dot)).astype(BF16)
            unturn(
                dq_ref,
                head * HD,
                dot(k_ref[:, :stop], score_grad, 1, 0) * 0.125,
                slice(start, stop),
            )
            dk = dot(q_ref[rows, start:stop], score_grad, 1, 1)
            dv = dot(grad, prob, 1, 1)
            for part in range(block + 1):
                a, b = split_tokens(tokens)[part]
                if key_grad[part] is None:
                    key_grad[part], value_grad[part] = dk[:, a:b], dv[:, a:b]
                else:
                    key_grad[part] = key_grad[part] + dk[:, a:b]
                    value_grad[part] = value_grad[part] + dv[:, a:b]
    for part, (a, b) in enumerate(split_tokens(tokens)):
        unturn(dk_ref, 0, key_grad[part], slice(a, b))
        dv_ref[:, a:b] = value_grad[part].astype(BF16)


def attend_back(prob, mixed, grad, qkv, cosine, sine):
    tokens = qkv.shape[1]
    heads = pl.BlockSpec((GROUP * HD, tokens), lambda i: (i, 0))
    one = pl.BlockSpec((HD, tokens), lambda i: (i, 0))
    table = pl.BlockSpec((HD // 2, tokens), lambda i: (0, 0))
    return pl.pallas_call(
        attend_back_kernel,
        grid=(KV_HEADS,),
        out_shape=(
            jax.ShapeDtypeStruct((HEADS * HD, tokens), BF16),
            jax.ShapeDtypeStruct((KV_HEADS * HD, tokens), BF16),
            jax.ShapeDtypeStruct((KV_HEADS * HD, tokens), BF16),
        ),
        in_specs=[
            pl.BlockSpec((GROUP, tokens, tokens), lambda i: (i, 0, 0)),
            heads,
            heads,
            heads,
            pl.BlockSpec((HD, tokens), lambda i: (HEADS + i, 0)),
            pl.BlockSpec((HD, tokens), lambda i: (HEADS + KV_HEADS + i, 0)),
            table,
            table,
        ],
        out_specs=(heads, one, one),
        compiler_params=pltpu.CompilerParams(vmem_limit_bytes=32 * MIB),
        cost_estimate=LONG,
        name="attend_back",
    )(prob, mixed, grad, qkv, qkv, qkv, cosine, sine)


def finish_grads_kernel(
    where_ref, normed_t_ref, dq_ref, dk_ref, dv_ref, out_grad_ref, keep_ref, send_ref, halves_ref
):
    normed_t = normed_t_ref[...]
    queries = dq_ref.shape[0]
    values = dv_ref.shape[0]
    halves_ref[0, :, :queries] = dot(normed_t, dq_ref[...], 1, 1).astype(BF16)
    halves_ref[0, :, queries:] = dot(normed_t, dk_ref[...], 1, 1).astype(BF16)
    halves_ref[1, :, :values] = dot(normed_t, dv_ref[...], 1, 1).astype(BF16)
    halves_ref[1, :, values:] = out_grad_ref[...]
    core = where_ref[3]
    keep_ref[...] = halves_ref[core]
    send_ref[...] = halves_ref[1 - core]


def finish_grads(where, normed_t, dq, dk, dv, out_grad):
    width = normed_t.shape[0]
    half = dq.shape[0] + dk.shape[0]
    shape = jax.ShapeDtypeStruct((width, half), BF16)
    vmem = pl.BlockSpec(memory_space=pltpu.VMEM)
    return pl.pallas_call(
        finish_grads_kernel,
        out_shape=(shape, shape),
        in_specs=[pl.BlockSpec(memory_space=pltpu.SMEM)] + [vmem] * 5,
        out_specs=(vmem, vmem),
        scratch_shapes=[pltpu.VMEM((2, width, half), BF16)],
        compiler_params=pltpu.CompilerParams(vmem_limit_bytes=24 * MIB),
        cost_estimate=LONG,
        name="finish_grads",
    )(where, normed_t, dq, dk, dv, out_grad)


def input_grad_kernel(dq_ref, dk_ref, dv_ref, weight_ref, tokens_ref, scale_ref, grad_ref, out_ref):
    queries, keys = dq_ref.shape[0], dk_ref.shape[0]
    end = queries + keys + dv_ref.shape[0]
    pull = dot(weight_ref[:, :queries], dq_ref[...], 1, 0)
    pull = pull + dot(weight_ref[:, queries : queries + keys], dk_ref[...], 1, 0)
    pull = pull + dot(weight_ref[:, queries + keys : end], dv_ref[...], 1, 0)
    values, scale = tokens_ref[...].astype(F32), scale_ref[...]
    mean = jnp.mean(pull * values, 0, keepdims=True)
    out_ref[...] = grad_ref[...] + scale * pull - values * (scale * scale * scale * mean)


def input_gradient(dq, dk, dv, weight, tokens, scale, grad):
    return pl.pallas_call(
        input_grad_kernel,
        out_shape=jax.ShapeDtypeStruct(grad.shape, F32),
        compiler_params=pltpu.CompilerParams(vmem_limit_bytes=24 * MIB),
        cost_estimate=SHORT,
        name="input_gradient",
    )(dq, dk, dv, weight, tokens, scale, grad)


def per_device(
    shards,
    tokens,
    segment_ids,
    positions,
    norm_attn,
    w_qkv,
    w_out,
    norm_mlp,
    w_gate_up,
    w_down,
    cotangent,
):
    rep, outer, mid, core = place()
    where = jnp.stack([rep, outer, mid, core]).astype(jnp.int32)
    count = shards // 4
    width = tokens.shape[1]
    rows = w_qkv.shape[0]
    kept = w_qkv.shape[1]
    units = w_gate_up.shape[1] // 8
    gain_attn, gain_mlp = norm_attn.astype(F32)[:, None], norm_mlp.astype(F32)[:, None]

    qkv_block = (w_qkv.astype(F32) * gain_attn).astype(BF16)
    tail = -kept % LANES
    attn_block = jnp.concatenate([qkv_block, w_out[:, width - tail :], w_out[:, : width - tail]], 1)
    feed_block = (w_gate_up.astype(F32) * gain_mlp).astype(BF16)
    part = attn_block.shape[1] // 4

    big = -(-units // (2 * LANES)) * LANES
    chunks = ((0, big), (big, units - big))

    def quarter(index):
        return jnp.concatenate(
            [lax.dynamic_slice(attn_block, (0, index * part), (rows, part))]
            + [
                lax.dynamic_slice(feed_block, (0, (kind * 4 + index) * units + start), (rows, size))
                for start, size in chunks
                for kind in range(2)
            ],
            1,
        )

    order = Order()
    mine = quarter(core * 2 + rep)
    other = hop(quarter((1 - core) * 2 + rep), shards, core_move)
    both = jnp.stack([mine, other])
    chip = jnp.concatenate([pick(both, core), pick(both, 1 - core)], 0)
    down_piece = pick(w_down.reshape(2, w_down.shape[0] // 2, width), rep)

    def outer_start(piece):
        return [piece] + [hop(piece, shards, outer_move(k, count)) for k in range(1, count)]

    def outer_stop(parts):
        return order.mark(jnp.stack(order.after(*parts)))

    def pair(held, came):
        return order.mark(jnp.stack(order.after(held, came)))

    def settled(held, came, by_rows=False):
        held, came = order.after(held, came)
        return order.mark(settle(held, came, where, by_rows))

    tokens_t, cot_t = tokens.T, cotangent.T

    attn_way = outer_start(order.mark(chip[:, :part]))
    cot_came = hop(cot_t, shards, core_move)
    half_dim = HD // 2
    freqs = ROPE_BASE ** (-2.0 * jnp.arange(half_dim, dtype=F32) / HD)
    angles = freqs[:, None] * positions[0].astype(F32)[None, :]
    cosine, sine = jnp.cos(angles), jnp.sin(angles)
    inputs = order.after(tokens_t).astype(F32)
    scale_attn = lax.rsqrt(jnp.mean(inputs * inputs, 0, keepdims=True) + EPSILON)
    normed_t = order.mark((inputs * scale_attn).astype(BF16))
    attn_own = outer_stop(attn_way)
    attn_way = hop(attn_own, shards, second_move)
    down_way = outer_start(order.after(down_piece))
    attn_own = pair(attn_own, attn_way)
    attn_way = hop(attn_own, shards, first_move)
    down_own = outer_stop(down_way)
    down_way = hop(down_own, shards, second_move)
    feed0_way = outer_start(order.after(chip[:, part : part + 2 * big]))
    attn_own = settled(attn_own, attn_way)
    attn_way = hop(attn_own, shards, core_move)
    down_own = pair(down_own, down_way)
    down_way = hop(down_own, shards, first_move)
    attn_own, attn_way = order.after(attn_own, attn_way)
    attn_full = order.mark(assemble(attn_own, attn_way, where))
    qkv = order.mark(project(order.after(normed_t), attn_full, cosine, sine))
    feed0_own = outer_stop(feed0_way)
    feed0_way = hop(feed0_own, shards, second_move)
    feed1_way = outer_start(order.after(chip[:, part + 2 * big :]))
    prob, mixed = attend(order.after(qkv), segment_ids[0])
    order.mark(mixed)
    down_own = settled(down_own, down_way, True)
    down_way = hop(down_own, shards, core_move)
    feed0_own = pair(feed0_own, feed0_way)
    feed0_way = hop(feed0_own, shards, first_move)
    feed1_own = outer_stop(feed1_way)
    feed1_way = hop(feed1_own, shards, second_move)
    after_attn, scale_mlp, mlp_low = branch(order.after(mixed), attn_full, tokens_t)
    order.mark(mlp_low)
    low_came = hop(mlp_low, shards, core_move)
    feed1_own = pair(feed1_own, feed1_way)
    feed1_way = hop(feed1_own, shards, first_move)
    feed0_full = settled(feed0_own, feed0_way)

    def run_feed(chunk, pieces, down_grad):
        pieces, low, cot, down = order.after(pieces, low_came, cot_came, down_way)
        return feed(
            where, chunks[chunk][0], (mlp_low, low), (cot_t, cot), pieces, (down_own, down), down_grad
        )

    sum0, sum0_other, back0, back0_other, feed0_grad, down_grad = run_feed(0, feed0_full, None)
    order.mark(feed0_grad)
    sum0_came = hop(sum0_other, shards, core_move)
    back0_came = hop(back0_other, shards, core_move)

    def feed_piece(array, to_mid, to_rep):
        array = array.reshape(2, count, 2, 2 * rows, array.shape[-1])
        return lax.dynamic_slice(
            array, (to_rep, 0, to_mid, 0, 0), (1, count, 1) + array.shape[3:]
        )[0, :, 0]

    feed0_sum = Reduction((feed0_grad,), feed_piece, shards)
    feed0_sum.first(order)
    feed1_full = settled(feed1_own, feed1_way)
    sum1, sum1_other, back1, back1_other, feed1_grad, down_grad = run_feed(1, feed1_full, down_grad)
    order.mark(feed1_grad)
    back1_came = hop(back1_other, shards, core_move)
    sum1_came = hop(sum1_other, shards, core_move)

    def down_piece_of(array, to_mid, to_rep):
        array = array.reshape(count // 2, 2, 2, 2, w_down.shape[0] // 2, width)
        return lax.dynamic_slice(
            array, (0, to_mid, 0, to_rep, 0, 0), (count // 2, 1, 2, 1) + array.shape[4:]
        )[:, 0, :, 0]

    feed1_sum = Reduction((feed1_grad,), feed_piece, shards)
    down_sum = Reduction((down_grad,), down_piece_of, shards)
    feed1_sum.first(order)
    backs = order.after(back0, back0_came, back1, back1_came)
    after_grad, mixed_grad, out_grad = return_branch(
        backs, after_attn, scale_mlp, cot_t, mixed, attn_full
    )
    order.mark(mixed_grad)
    feed0_sum.second(order)
    dq, dk, dv = attend_back(prob, mixed, order.after(mixed_grad), qkv, cosine, sine)
    order.mark(dq)
    feed1_sum.second(order)
    down_sum.first(order)
    feed0_total = feed0_sum.third(order)
    keep_attn, send_attn = finish_grads(where, normed_t, order.after(dq), dk, dv, out_grad)
    order.mark(keep_attn)

    def attn_piece(array, to_mid, to_rep):
        array = array.reshape(count, 2, 2 * rows, 2 * part)
        return lax.dynamic_slice(
            array, (0, to_mid, 0, to_rep * part), (count, 1, 2 * rows, part)
        )[:, 0]

    attn_came = hop(send_attn, shards, core_move)
    input_grad = input_gradient(order.after(dq), dk, dv, attn_full, tokens_t, scale_attn, after_grad)
    order.mark(input_grad)
    attn_sum = Reduction((keep_attn, attn_came), attn_piece, shards)
    attn_sum.first(order)
    down_sum.second(order)
    feed1_total = feed1_sum.third(order)
    feed_way = send_outer(
        order.mark(jnp.concatenate(order.after(feed0_total, feed1_total), -1)), shards
    )
    output = after_attn + (sum0 + sum1)
    output = (output + (sum0_came.astype(F32) + sum1_came.astype(F32))).astype(BF16)
    attn_sum.second(order)
    down_total = down_sum.third(order)
    down_way = send_down(down_total, shards)
    feed_total = order.mark(add_low(*order.after(*feed_way)))
    feed_quarters = share_columns(feed_total, shards)
    attn_total = attn_sum.third(order)
    attn_way = send_outer(attn_total, shards)
    down_total = order.mark(add_low(*order.after(*down_way)))
    grad_down = share_down(down_total, shards).astype(F32)
    attn_quarters = share_columns(add_low(*order.after(*attn_way)), shards)

    attn_rows = jnp.concatenate(attn_quarters, 1).astype(F32)
    feed_rows = jnp.concatenate(
        [
            q[:, 2 * start + kind * size : 2 * start + (kind + 1) * size]
            for kind in range(2)
            for q in feed_quarters
            for start, size in chunks
        ],
        1,
    ).astype(F32)
    qkv_rows = attn_rows[:, :kept]
    grad_norm_attn = jnp.sum(qkv_rows * w_qkv.astype(F32), 1)
    grad_norm_mlp = jnp.sum(feed_rows * w_gate_up.astype(F32), 1)
    grad_out = jnp.concatenate([attn_rows[:, kept + tail :], attn_rows[:, kept : kept + tail]], 1)
    return (
        output.T,
        input_grad.T,
        grad_norm_attn,
        qkv_rows * gain_attn,
        grad_out,
        grad_norm_mlp,
        feed_rows * gain_mlp,
        grad_down,
    )


def solution(mesh):
    in_specs = (
        P(("rep", "shard"), None),
        P(("rep", "shard"), None),
        P(("rep", "shard"), None),
        P("shard"),
        P("shard", None),
        P("shard", None),
        P("shard"),
        P("shard", None),
        P("shard", None),
        P(("rep", "shard"), None),
    )
    out_specs = (
        P(("rep", "shard"), None),
        P(("rep", "shard"), None),
        P("shard"),
        P("shard", None),
        P("shard", None),
        P("shard"),
        P("shard", None),
        P("shard", None),
    )
    return jax.shard_map(
        functools.partial(per_device, mesh.shape["shard"]),
        mesh=mesh,
        in_specs=in_specs,
        out_specs=out_specs,
        check_vma=False,
    )
```

time: 834 us -> 357 us (0.43)
  blocking collectives: 404 us -> 0 us
  matrix products: 111 us -> 0 us
  Pallas kernels: 0 us -> 89.7 us
  waiting for transfers between devices: 170 us -> 92.5 us
  starting transfers between devices: 32.8 us -> 79.3 us
  local copies, waits for them, and re-layouts: 49.7 us -> 30.7 us
  other arithmetic: 38.8 us -> 55.6 us
  between operations: 17 us -> 2.13 us
    unnamed x3 -> x0, blocking collectives: 399 us -> none
    all_gather x4 -> x0, waiting for transfers between devices: 133 us -> none  [the longest x1 56 us: per_device(): lax.all_gather(w_gate_up, 'shard', axis=0, tiled=True)]
    dot_general x18 -> x0, matrix products: 111 us -> none  [the longest x1 12.5 us: per_device(): jnp.einsum('tf,df->td', gate_up_grad, lax.all_gather(w_gate_up, 'shard',...]
    ppermute x0 -> x55, waiting for transfers between devices: none -> 92.5 us  [the longest x52 84.7 us: hop(): return lax.ppermute(values, AXES, pairs)]
    pallas_call x0 -> x14, Pallas kernels: none -> 89.7 us  [the longest x2 34.7 us: feed(): pl.pallas_call(body, in_specs=[pl.BlockSpec(memory_space=pltpu.SMEM)] + [...]
    ppermute x0 -> x55, starting transfers between devices: none -> 79.3 us  [the longest x52 74.2 us: hop(): return lax.ppermute(values, AXES, pairs)]
    psum x1 -> x0, waiting for transfers between devices: 34.5 us -> none  [per_device(): lax.psum(shard_sums[0].astype(jnp.bfloat16), 'rep').astype(jnp.float32)]
    unnamed x3 -> x0, starting transfers between devices: 32.6 us -> none
  transfers between devices with their start and end apart: 9 -> 55, of which waited for: 4 -> 20; matrix products, arithmetic and copies ran while one was open for 61% -> 16% of each run, Pallas kernels for 0% -> 18%
where the time goes in v2:
time: 357 us; the launch traced here: 350 us
  waiting for transfers between devices  92.5 us (26%)
  Pallas kernels  89.7 us (25%)
  starting transfers between devices  79.3 us (22%)
  other arithmetic  55.6 us (16%)
  local copies, waits for them, and re-layouts  30.7 us (9%)
    ppermute x52, waiting for transfers between devices, hop(): return lax.ppermute(values, AXES, pairs)  84.7 us
    ppermute x52, starting transfers between devices, hop(): return lax.ppermute(values, AXES, pairs)  74.2 us
    pallas_call x2, Pallas kernels, feed(): pl.pallas_call(body, in_specs=[pl.BlockSpec(memory_space=pltpu.SMEM)] + [...  34.7 us
    unnamed x114, local copies, waits for them, and re-layouts  24 us
    convert_element_type x12, other arithmetic, add_low(): return total.astype(BF16)  18.4 us
    pallas_call x4, Pallas kernels, settle(): pl.pallas_call(functools.partial(settle_kernel, by_rows), out_shape=jax.S...  13.5 us
    pallas_call x1, Pallas kernels, attend(): pl.pallas_call(attend_kernel, grid=(KV_HEADS,), out_shape=(jax.ShapeDtype...  11.2 us
    pallas_call x1, Pallas kernels, attend_back(): pl.pallas_call(attend_back_kernel, grid=(KV_HEADS,), out_shape=(jax.Shape...  9.52 us
  transfers between devices with their start and end apart: 55, of which 20 were waited for; matrix products, arithmetic and copies ran while one was open for 16% of the time, Pallas kernels for 18%

profile of v2, /device:TPU:0, one launch (start us, length us, event | category | flops | bytes accessed | tf_op | source)
XLA Modules:
  0.0 349.9 jit_solution(15703160749713601376)
XLA Ops:
  6.6 3.0 collective-permute-start.1
  9.6 2.6 collective-permute-start.2
  14.0 2.5 collective-permute-done.1
  16.5 6.1 %collective-permute-done.2 = bf16[120,640]{1,0:T(8,128)(2,1)S(1)} collective-permute-done((bf16[120,640]{1,0:T(8,128)(2,1)S(1)}, bf16[120,640]{1,0:T(8,128)(2,1)S(1)}, u32[]{:S(2)}, u32[]{:S(2)}) %collective-permute-start.2) | collective-permute-done | bytes 153632 | tf_op jit(solution)/shard_map/ppermute | solution.py:39
  24.3 8.6 %collective-permute-done.4 = bf16[4,120,640]{2,1,0:T(8,128)(2,1)S(1)} collective-permute-done((bf16[4,120,640]{2,1,0:T(8,128)(2,1)S(1)}, bf16[4,120,640]{2,1,0:T(8,128)(2,1)S(1)}, u32[]{:S(2)}, u32[]{:S(2)}) %collective-permute-start.4) | collective-permute-done | bytes 614432 | tf_op jit(solution)/shard_map/ppermute | solution.py:39
  35.3 3.8 %collective-permute-start.6 = (bf16[80,960]{1,0:T(8,128)(2,1)}, bf16[80,960]{1,0:T(8,128)(2,1)S(1)}, u32[]{:S(2)}, u32[]{:S(2)}) collective-permute-start(bf16[80,960]{1,0:T(8,128)(2,1)} %dynamic-slice_bitcast_fusion.20), channel_id=1, source_target_pairs={{0,4},{1,5},{2,6},{3,7},{4,8},{5,9},{6,10},{7,11},{8,12},{9,13},{1... | collective-permute-start | bytes 460808 | tf_op jit(solution)/shard_map/ppermute | solution.py:39
  39.1 1.6 collective-permute-start.7
  41.5 4.0 %collective-permute-done.6 = bf16[80,960]{1,0:T(8,128)(2,1)S(1)} collective-permute-done((bf16[80,960]{1,0:T(8,128)(2,1)}, bf16[80,960]{1,0:T(8,128)(2,1)S(1)}, u32[]{:S(2)}, u32[]{:S(2)}) %collective-permute-start.6) | collective-permute-done | bytes 153632 | tf_op jit(solution)/shard_map/ppermute | solution.py:39
  45.5 4.6 %collective-permute-done.7 = bf16[80,960]{1,0:T(8,128)(2,1)} collective-permute-done((bf16[80,960]{1,0:T(8,128)(2,1)}, bf16[80,960]{1,0:T(8,128)(2,1)}, u32[]{:S(2)}, u32[]{:S(2)}) %collective-permute-start.7) | collective-permute-done | bytes 153632 | tf_op jit(solution)/shard_map/ppermute | solution.py:39
  50.1 2.0 pad_maximum_fusion.9
  52.1 4.9 %settle.4 = bf16[2,4,2,120,640]{4,3,2,1,0:T(8,128)(2,1)} custom-call(s32[4]{0:T(128)S(1)} %pad_add_fusion.where_ref, bf16[2,4,120,640]{3,2,1,0:T(8,128)(2,1)S(1)} %pad_maximum_fusion.4.held_ref, bf16[2,4,120,640]{3,2,1,0:T(8,128)(2,1)} %collective-permute-done.5.came_ref), custom_call_target="tpu_custom_call" | custom-call | flops 1000000 | tf_op jit(solution)/shard_map/settle/pallas_call | solution.py:106
  60.9 1.6 fusion.25
  62.6 4.0 %collective-permute-start.11 = (bf16[120,768]{1,0:T(8,128)(2,1)}, bf16[120,768]{1,0:T(8,128)(2,1)}, u32[]{:S(2)}, u32[]{:S(2)}) collective-permute-start(bf16[120,768]{1,0:T(8,128)(2,1)} %fusion.25), channel_id=1, source_target_pairs={{0,4},{1,5},{2,6},{3,7},{4,8},{5,9},{6,10},{7,11},{8,12},{9,13},{1... | collective-permute-start | bytes 552968 | tf_op jit(solution)/shard_map/ppermute | solution.py:39
  66.5 2.0 collective-permute-start.12
  68.5 4.8 %collective-permute-start.13 = (bf16[120,768]{1,0:T(8,128)(2,1)}, bf16[120,768]{1,0:T(8,128)(2,1)}, u32[]{:S(2)}, u32[]{:S(2)}) collective-permute-start(bf16[120,768]{1,0:T(8,128)(2,1)} %fusion.25), channel_id=1, source_target_pairs={{0,12},{1,13},{2,14},{3,15},{4,0},{5,1},{6,2},{7,3},{8,4},{9,5},{1... | collective-permute-start | bytes 552968 | tf_op jit(solution)/shard_map/ppermute | solution.py:39
  73.4 2.3 pad_maximum_fusion.2.held_ref
  77.2 2.9 assemble.1.weight_ref.refs_8_
  80.1 1.9 project.1.q_ref.k_ref.v_ref
  82.4 2.7 pad_maximum_fusion.8
  85.6 2.9 collective-permute-start.14
  89.5 11.2 %attend.1 = (bf16[15,512,512]{2,1,0:T(8,128)(2,1)S(1)}, bf16[960,512]{1,0:T(8,128)(2,1)S(1)}) custom-call(s32[1,512]{1,0:T(1,128)S(1)} %copy-done.28, s32[512,1]{1,0:T(8,128)S(1)} %copy.28.seg_col_ref, bf16[1600,512]{1,0:T(8,128)(2,1)S(1)} %project.1.q_ref.k_ref.v_ref, bf16[1600,512]{1,0:T(8,128)(2,1)S(1)} %project.1.q_ref.k_ref.v_ref, ...), custom_call_target="tpu_custom_call" | custom-call | flops 199999995904 | tf_op jit(solution)/shard_map/attend/pallas_call | solution.py:330
  100.7 3.1 copy-done.30
  103.8 1.9 collective-permute-start.16
  105.7 4.1 %settle.5 = bf16[4,2,2,80,960]{4,3,2,1,0:T(8,128)(2,1)} custom-call(s32[4]{0:T(128)S(1)} %pad_add_fusion.where_ref, bf16[2,4,80,960]{3,2,1,0:T(8,128)(2,1)} %pad_maximum_fusion.2.held_ref, bf16[2,4,80,960]{3,2,1,0:T(8,128)(2,1)} %collective-permute-done.18.came_ref), custom_call_target="tpu_custom_call" | custom-call | flops 1000000 | tf_op jit(solution)/shard_map/settle/pallas_call | solution.py:106
  109.8 2.6 pad_maximum_fusion.held_ref
  113.9 1.9 pad_maximum_fusion.12
  115.8 1.6 branch.1
  119.5 13.7 %collective-permute-done.20 = bf16[4,120,512]{2,1,0:T(8,128)(2,1)} collective-permute-done((bf16[4,120,512]{2,1,0:T(8,128)(2,1)}, bf16[4,120,512]{2,1,0:T(8,128)(2,1)}, u32[]{:S(2)}, u32[]{:S(2)}) %collective-permute-start.20) | collective-permute-done | bytes 491552 | tf_op jit(solution)/shard_map/ppermute | solution.py:39
  133.2 2.2 pad_maximum_fusion.6.held_ref
  137.4 2.4 settle.6
  139.8 1.7 copy-done.7
  141.5 20.4 %feed.2 = (f32[960,512]{1,0:T(8,128)}, bf16[960,512]{1,0:T(8,128)(2,1)}, f32[960,512]{1,0:T(8,128)}, bf16[960,512]{1,0:T(8,128)(2,1)S(1)}, bf16[2,960,768]{2,1,0:T(8,128)(2,1)}, /*index=5*/bf16[2,640,960]{2,1,0:T(8,128)(2,1)}) custom-call(s32[4]{0:T(128)S(1)} %pad_add_fusion.where_ref, bf16[960,512]{1,0:T(8,128)(2,1)} %copy-done.29, ...), custom_call_target="tpu_custom_call" | custom-call | flops 199999995904 | tf_op jit(solution)/shard_map/feed/pallas_call | solution.py:555
  164.6 2.1 settle.7
  168.0 14.3 %feed.3 = (f32[960,512]{1,0:T(8,128)}, bf16[960,512]{1,0:T(8,128)(2,1)}, f32[960,512]{1,0:T(8,128)}, bf16[960,512]{1,0:T(8,128)(2,1)}, bf16[2,960,512]{2,1,0:T(8,128)(2,1)}, /*index=5*/bf16[2,640,960]{2,1,0:T(8,128)(2,1)}) custom-call(s32[4]{0:T(128)S(1)} %pad_add_fusion.where_ref, bf16[960,512]{1,0:T(8,128)(2,1)} %copy-done.29, ...), custom_call_target="tpu_custom_call", output_to_operand_aliasing={{5}: (8, {})} | custom-call | flops 199999995904 | tf_op jit(solution)/shard_map/feed/pallas_call | solution.py:555
  187.9 2.4 copy-done.4
  193.0 5.7 %return_branch.1 = (f32[960,512]{1,0:T(8,128)S(1)}, bf16[960,512]{1,0:T(8,128)(2,1)S(1)}, bf16[960,960]{1,0:T(8,128)(2,1)S(1)}) custom-call(f32[960,512]{1,0:T(8,128)S(1)} %copy-done.32, bf16[960,512]{1,0:T(8,128)(2,1)} %collective-permute-done.27.refs_1_, f32[960,512]{1,0:T(8,128)S(1)} %copy-done.33, bf16[960,512]{1,0:T(8,128)(2,1)} %collective-permute-done.28.refs_3_, ...), custom_call_target="tpu_custom_call" | custom-call | flops 199999995904 | tf_op jit(solution)/shard_map/return_branch/pallas_call | solution.py:611
  198.8 3.8 %collective-permute-done.29 = bf16[2,4,120,768]{3,2,1,0:T(8,128)(2,1)} collective-permute-done((bf16[2,4,120,768]{3,2,1,0:T(8,128)(2,1)}, bf16[2,4,120,768]{3,2,1,0:T(8,128)(2,1)}, u32[]{:S(2)}, u32[]{:S(2)}) %collective-permute-start.29) | collective-permute-done | bytes 1474592 | tf_op jit(solution)/shard_map/ppermute | solution.py:39
  202.6 2.4 fusion.4
  206.2 3.2 copy-done.31
  209.4 9.5 %attend_back.1 = (bf16[960,512]{1,0:T(8,128)(2,1)S(1)}, bf16[320,512]{1,0:T(8,128)(2,1)S(1)}, bf16[320,512]{1,0:T(8,128)(2,1)S(1)}) custom-call(bf16[15,512,512]{2,1,0:T(8,128)(2,1)S(1)} %copy-done.31, bf16[960,512]{1,0:T(8,128)(2,1)S(1)} %copy-done.35, bf16[960,512]{1,0:T(8,128)(2,1)S(1)} %get-tuple-element.185.grad_ref, bf16[1600,512]{1,0:T(8,128)(2,1)S(1)} %copy-done.17, ...), custom_call_target="tpu_custom_call" | custom-call | flops 199999995904 | tf_op jit(solution)/shard_map/attend_back/pallas_call | solution.py:673
  219.1 2.1 fusion.16
  223.8 2.7 fusion.3
  226.5 4.6 %finish_grads.1 = (bf16[960,1280]{1,0:T(8,128)(2,1)S(1)}, bf16[960,1280]{1,0:T(8,128)(2,1)}) custom-call(s32[4]{0:T(128)S(1)} %copy-done.27, bf16[960,512]{1,0:T(8,128)(2,1)S(1)} %fusion.1.normed_ref.normed_t_ref, bf16[960,512]{1,0:T(8,128)(2,1)S(1)} %get-tuple-element.196.dq_ref, bf16[320,512]{1,0:T(8,128)(2,1)S(1)} %get-tuple-element.192.dk_ref, ...), custom_call_target="tpu_custom_call" | custom-call | flops 199999995904 | tf_op jit(solution)/shard_map/finish_grads/pallas_call | solution.py:718
  234.8 2.4 copy-done.5
  239.7 4.0 %input_gradient.1 = f32[960,512]{1,0:T(8,128)} custom-call(bf16[960,512]{1,0:T(8,128)(2,1)S(1)} %get-tuple-element.196.dq_ref, bf16[320,512]{1,0:T(8,128)(2,1)S(1)} %get-tuple-element.192.dk_ref, bf16[320,512]{1,0:T(8,128)(2,1)S(1)} %copy-done.19, bf16[960,2560]{1,0:T(8,128)(2,1)S(1)} %copy-done.5, bf16[960,512]{1,0:T(8,128)(2,1)S(1)} %bitcast.200, ...), custom_call_target="tpu_custom_call" | custom-call | flops 1000000 | tf_op jit(solution)/shard_map/input_gradient/pallas_call | solution.py:742
  243.7 1.6 fusion.17
  247.4 8.3 %collective-permute-done.35 = bf16[2,2,2,80,960]{4,3,2,1,0:T(8,128)(2,1)} collective-permute-done((bf16[2,2,2,80,960]{4,3,2,1,0:T(8,128)(2,1)}, bf16[2,2,2,80,960]{4,3,2,1,0:T(8,128)(2,1)}, u32[]{:S(2)}, u32[]{:S(2)}) %collective-permute-start.35) | collective-permute-done | bytes 1228832 | tf_op jit(solution)/shard_map/ppermute | solution.py:39
  260.6 2.0 collective-permute-start.38
  262.7 13.2 %collective-permute-done.33 = bf16[2,4,120,640]{3,2,1,0:T(8,128)(2,1)} collective-permute-done((bf16[2,4,120,640]{3,2,1,0:T(8,128)(2,1)}, bf16[2,4,120,640]{3,2,1,0:T(8,128)(2,1)}, u32[]{:S(2)}, u32[]{:S(2)}) %collective-permute-start.33) | collective-permute-done | bytes 1228832 | tf_op jit(solution)/shard_map/ppermute | solution.py:39
  275.8 2.3 collective-permute-start.39
  278.1 2.3 fusion.10
  280.4 1.6 fusion.8
  282.1 2.0 collective-permute-done.38
  284.1 5.8 %collective-permute-done.39 = bf16[120,1280]{1,0:T(8,128)(2,1)S(1)} collective-permute-done((bf16[120,1280]{1,0:T(8,128)(2,1)S(1)}, bf16[120,1280]{1,0:T(8,128)(2,1)S(1)}, u32[]{:S(2)}, u32[]{:S(2)}) %collective-permute-start.39) | collective-permute-done | bytes 307232 | tf_op jit(solution)/shard_map/ppermute | solution.py:39
  294.1 5.2 %fusion.13 = bf16[512,960]{0,1:T(8,128)(2,1)} fusion(bf16[960,512]{1,0:T(8,128)(2,1)} %collective-permute-done.26, bf16[960,512]{1,0:T(8,128)(2,1)} %collective-permute-done.25, f32[960,512]{1,0:T(8,128)} %copy-done.13, f32[960,512]{1,0:T(8,128)} %get-tuple-element.160, f32[960,512]{1,0:T(8,128)} %get-tuple-element.169), kind=kLoop, calls=%fused_computation.33 | loop fusion | flops 3440640 | bytes 8847360 | tf_op jit(solution)/shard_map/transpose | solution.py:949
  300.3 2.5 collective-permute-start.44
  306.6 1.9 convert_multiply_fusion.2
  309.4 1.6 fusion.12
  311.1 3.5 collective-permute-done.44
  314.6 4.3 %collective-permute-done.45 = bf16[2,80,960]{2,1,0:T(8,128)(2,1)S(1)} collective-permute-done((bf16[2,80,960]{2,1,0:T(8,128)(2,1)S(1)}, bf16[2,80,960]{2,1,0:T(8,128)(2,1)S(1)}, u32[]{:S(2)}, u32[]{:S(2)}) %collective-permute-start.45) | collective-permute-done | bytes 307232 | tf_op jit(solution)/shard_map/ppermute | solution.py:235
  318.9 11.9 %collective-permute-start.41 = (bf16[120,640]{1,0:T(8,128)(2,1)S(1)}, bf16[120,640]{1,0:T(8,128)(2,1)S(1)}, u32[]{:S(2)}, u32[]{:S(2)}) collective-permute-start(bf16[120,640]{1,0:T(8,128)(2,1)S(1)} %get-tuple-element.254), channel_id=1, source_target_pairs={{0,4},{1,5},{2,6},{3,7},{4,8},{5,9},{6,10},{7,11},{8,12},{9,13},{1... | collective-permute-start | bytes 460808 | tf_op jit(solution)/shard_map/ppermute | solution.py:39
  330.8 2.4 collective-permute-start.43
  333.6 4.5 %collective-permute-done.42 = bf16[120,640]{1,0:T(8,128)(2,1)S(1)} collective-permute-done((bf16[120,640]{1,0:T(8,128)(2,1)S(1)}, bf16[120,640]{1,0:T(8,128)(2,1)S(1)}, u32[]{:S(2)}, u32[]{:S(2)}) %collective-permute-start.42) | collective-permute-done | bytes 153632 | tf_op jit(solution)/shard_map/ppermute | solution.py:39
  341.7 3.7 %collective-permute-done.47 = bf16[60,640]{1,0:T(8,128)(2,1)S(1)} collective-permute-done((bf16[60,640]{1,0:T(8,128)(2,1)S(1)}, bf16[60,640]{1,0:T(8,128)(2,1)S(1)}, u32[]{:S(2)}, u32[]{:S(2)}) %collective-permute-start.47) | collective-permute-done | bytes 76832 | tf_op jit(solution)/shard_map/ppermute | solution.py:39
  (248 shorter events, 72.2 us)
Async XLA Ops:
  0.6 34.0 %copy-start = (bf16[160,960]{1,0:T(8,128)(2,1)S(1)}, bf16[160,960]{1,0:T(8,128)(2,1)}, u32[]{:S(2)}) copy-start(bf16[160,960]{1,0:T(8,128)(2,1)} %param.18) | copy-start | bytes 921604
  4.7 1.7 collective-permute-start
  6.6 9.9 %collective-permute-start.1 = (bf16[120,640]{1,0:T(8,128)(2,1)S(1)}, bf16[120,640]{1,0:T(8,128)(2,1)S(1)}, u32[]{:S(2)}, u32[]{:S(2)}) collective-permute-start(bf16[120,640]{1,0:T(8,128)(2,1)S(1)} %fusion.30), channel_id=1, source_target_pairs={{0,4},{1,5},{2,6},{3,7},{4,8},{5,9},{6,10},{7,11},{8,12},{9,13},{1... | collective-permute-start | bytes 460808 | tf_op jit(solution)/shard_map/ppermute | solution.py:39
  9.6 13.0 %collective-permute-start.2 = (bf16[120,640]{1,0:T(8,128)(2,1)S(1)}, bf16[120,640]{1,0:T(8,128)(2,1)S(1)}, u32[]{:S(2)}, u32[]{:S(2)}) collective-permute-start(bf16[120,640]{1,0:T(8,128)(2,1)S(1)} %fusion.30), channel_id=1, source_target_pairs={{0,8},{1,9},{2,10},{3,11},{4,12},{5,13},{6,14},{7,15},{8,0},{9,1},... | collective-permute-start | bytes 460808 | tf_op jit(solution)/shard_map/ppermute | solution.py:39
  12.2 10.4 %collective-permute-start.3 = (bf16[120,640]{1,0:T(8,128)(2,1)S(1)}, bf16[120,640]{1,0:T(8,128)(2,1)S(1)}, u32[]{:S(2)}, u32[]{:S(2)}) collective-permute-start(bf16[120,640]{1,0:T(8,128)(2,1)S(1)} %fusion.30), channel_id=1, source_target_pairs={{0,12},{1,13},{2,14},{3,15},{4,0},{5,1},{6,2},{7,3},{8,4},{9,5},{1... | collective-permute-start | bytes 460808 | tf_op jit(solution)/shard_map/ppermute | solution.py:39
  22.7 10.2 %collective-permute-start.4 = (bf16[4,120,640]{2,1,0:T(8,128)(2,1)S(1)}, bf16[4,120,640]{2,1,0:T(8,128)(2,1)S(1)}, u32[]{:S(2)}, u32[]{:S(2)}) collective-permute-start(bf16[4,120,640]{2,1,0:T(8,128)(2,1)S(1)} %pad_maximum_fusion.11), channel_id=1, source_target_pairs={{0,16},{1,3},{2,18},{3,1},{4,20},{5,7},{6,22},{7,5},{8,24},{9,11},... | collective-permute-start | bytes 1843208 | tf_op jit(solution)/shard_map/ppermute | solution.py:39
  33.1 19.1 %collective-permute-start.5 = (bf16[2,4,120,640]{3,2,1,0:T(8,128)(2,1)S(1)}, bf16[2,4,120,640]{3,2,1,0:T(8,128)(2,1)}, u32[]{:S(2)}, u32[]{:S(2)}) collective-permute-start(bf16[2,4,120,640]{3,2,1,0:T(8,128)(2,1)S(1)} %pad_maximum_fusion.4.held_ref), channel_id=1, source_target_pairs={{0,2},{1,17},{2,0},{3,19},{4,6},{5,21},{6,4},{7,23},{8,10},{9,25},... | collective-permute-start | bytes 3686408 | tf_op jit(solution)/shard_map/ppermute | solution.py:39
  35.3 10.2 %collective-permute-start.6 = (bf16[80,960]{1,0:T(8,128)(2,1)}, bf16[80,960]{1,0:T(8,128)(2,1)S(1)}, u32[]{:S(2)}, u32[]{:S(2)}) collective-permute-start(bf16[80,960]{1,0:T(8,128)(2,1)} %dynamic-slice_bitcast_fusion.20), channel_id=1, source_target_pairs={{0,4},{1,5},{2,6},{3,7},{4,8},{5,9},{6,10},{7,11},{8,12},{9,13},{1... | collective-permute-start | bytes 460808 | tf_op jit(solution)/shard_map/ppermute | solution.py:39
  39.1 11.1 %collective-permute-start.7 = (bf16[80,960]{1,0:T(8,128)(2,1)}, bf16[80,960]{1,0:T(8,128)(2,1)}, u32[]{:S(2)}, u32[]{:S(2)}) collective-permute-start(bf16[80,960]{1,0:T(8,128)(2,1)} %dynamic-slice_bitcast_fusion.20), channel_id=1, source_target_pairs={{0,8},{1,9},{2,10},{3,11},{4,12},{5,13},{6,14},{7,15},{8,0},{9,1},... | collective-permute-start | bytes 460808 | tf_op jit(solution)/shard_map/ppermute | solution.py:39
  40.7 9.4 %collective-permute-start.8 = (bf16[80,960]{1,0:T(8,128)(2,1)}, bf16[80,960]{1,0:T(8,128)(2,1)}, u32[]{:S(2)}, u32[]{:S(2)}) collective-permute-start(bf16[80,960]{1,0:T(8,128)(2,1)} %dynamic-slice_bitcast_fusion.20), channel_id=1, source_target_pairs={{0,12},{1,13},{2,14},{3,15},{4,0},{5,1},{6,2},{7,3},{8,4},{9,5},{1... | collective-permute-start | bytes 460808 | tf_op jit(solution)/shard_map/ppermute | solution.py:39
  41.5 126.5 %copy-start.26 = (s32[4]{0:T(128)}, s32[4]{0:T(128)S(1)}, u32[]{:S(2)}) copy-start(s32[4]{0:T(128)S(1)} %pad_add_fusion.where_ref) | copy-start | bytes 52
  57.0 18.6 %collective-permute-start.9 = (bf16[2,4,240,640]{3,2,1,0:T(8,128)(2,1)}, bf16[2,4,240,640]{3,2,1,0:T(8,128)(2,1)}, u32[]{:S(2)}, u32[]{:S(2)}) collective-permute-start(bf16[2,4,240,640]{3,2,1,0:T(8,128)(2,1)} %bitcast.22.own_ref), channel_id=1, source_target_pairs={{0,1},{1,0},{2,3},{3,2},{4,5},{5,4},{6,7},{7,6},{8,9},{9,8},{10,11... | collective-permute-start | bytes 7372808 | tf_op jit(solution)/shard_map/ppermute | solution.py:39
  57.1 11.4 %collective-permute-start.10 = (bf16[4,80,960]{2,1,0:T(8,128)(2,1)}, bf16[4,80,960]{2,1,0:T(8,128)(2,1)S(1)}, u32[]{:S(2)}, u32[]{:S(2)}) collective-permute-start(bf16[4,80,960]{2,1,0:T(8,128)(2,1)} %pad_maximum_fusion.9), channel_id=1, source_target_pairs={{0,16},{1,3},{2,18},{3,1},{4,20},{5,7},{6,22},{7,5},{8,24},{9,11},... | collective-permute-start | bytes 1843208 | tf_op jit(solution)/shard_map/ppermute | solution.py:39
  58.6 82.9 %collective-permute-start.22 = (bf16[960,512]{1,0:T(8,128)(2,1)}, bf16[960,512]{1,0:T(8,128)(2,1)}, u32[]{:S(2)}, u32[]{:S(2)}) collective-permute-start(bf16[960,512]{1,0:T(8,128)(2,1)} %bitcast.40.refs_2_.refs_6_), channel_id=1, source_target_pairs={{0,1},{1,0},{2,3},{3,2},{4,5},{5,4},{6,7},{7,6},{8,9},{9,8},{10,11... | collective-permute-start | bytes 2949128 | tf_op jit(solution)/shard_map/ppermute | solution.py:39
  59.3 20.8 %copy-start.20 = (f32[32,512]{1,0:T(8,128)}, f32[32,512]{1,0:T(8,128)S(1)}, u32[]{:S(2)}) copy-start(f32[32,512]{1,0:T(8,128)S(1)} %get-tuple-element.270.sin_ref) | copy-start | bytes 196612
  59.3 20.8 %copy-start.22 = (f32[32,512]{1,0:T(8,128)}, f32[32,512]{1,0:T(8,128)S(1)}, u32[]{:S(2)}) copy-start(f32[32,512]{1,0:T(8,128)S(1)} %get-tuple-element.271.cos_ref) | copy-start | bytes 196612
  62.6 19.8 %collective-permute-start.11 = (bf16[120,768]{1,0:T(8,128)(2,1)}, bf16[120,768]{1,0:T(8,128)(2,1)}, u32[]{:S(2)}, u32[]{:S(2)}) collective-permute-start(bf16[120,768]{1,0:T(8,128)(2,1)} %fusion.25), channel_id=1, source_target_pairs={{0,4},{1,5},{2,6},{3,7},{4,8},{5,9},{6,10},{7,11},{8,12},{9,13},{1... | collective-permute-start | bytes 552968 | tf_op jit(solution)/shard_map/ppermute | solution.py:39
  66.5 15.8 %collective-permute-start.12 = (bf16[120,768]{1,0:T(8,128)(2,1)}, bf16[120,768]{1,0:T(8,128)(2,1)}, u32[]{:S(2)}, u32[]{:S(2)}) collective-permute-start(bf16[120,768]{1,0:T(8,128)(2,1)} %fusion.25), channel_id=1, source_target_pairs={{0,8},{1,9},{2,10},{3,11},{4,12},{5,13},{6,14},{7,15},{8,0},{9,1},... | collective-permute-start | bytes 552968 | tf_op jit(solution)/shard_map/ppermute | solution.py:39
  68.5 13.8 %collective-permute-start.13 = (bf16[120,768]{1,0:T(8,128)(2,1)}, bf16[120,768]{1,0:T(8,128)(2,1)}, u32[]{:S(2)}, u32[]{:S(2)}) collective-permute-start(bf16[120,768]{1,0:T(8,128)(2,1)} %fusion.25), channel_id=1, source_target_pairs={{0,12},{1,13},{2,14},{3,15},{4,0},{5,1},{6,2},{7,3},{8,4},{9,5},{1... | collective-permute-start | bytes 552968 | tf_op jit(solution)/shard_map/ppermute | solution.py:39
  75.7 28.1 %collective-permute-start.18 = (bf16[2,4,80,960]{3,2,1,0:T(8,128)(2,1)}, bf16[2,4,80,960]{3,2,1,0:T(8,128)(2,1)}, u32[]{:S(2)}, u32[]{:S(2)}) collective-permute-start(bf16[2,4,80,960]{3,2,1,0:T(8,128)(2,1)} %pad_maximum_fusion.2.held_ref), channel_id=1, source_target_pairs={{0,2},{1,17},{2,0},{3,19},{4,6},{5,21},{6,4},{7,23},{8,10},{9,25},... | collective-permute-start | bytes 3686408 | tf_op jit(solution)/shard_map/ppermute | solution.py:39
  82.3 18.3 %copy-start.16 = (bf16[1600,512]{1,0:T(8,128)(2,1)}, bf16[1600,512]{1,0:T(8,128)(2,1)S(1)}, u32[]{:S(2)}) copy-start(bf16[1600,512]{1,0:T(8,128)(2,1)S(1)} %project.1.q_ref.k_ref.v_ref) | copy-start | bytes 4915204
  85.1 24.7 %collective-permute-start.17 = (bf16[4,120,768]{2,1,0:T(8,128)(2,1)}, bf16[4,120,768]{2,1,0:T(8,128)(2,1)}, u32[]{:S(2)}, u32[]{:S(2)}) collective-permute-start(bf16[4,120,768]{2,1,0:T(8,128)(2,1)} %pad_maximum_fusion.8), channel_id=1, source_target_pairs={{0,16},{1,3},{2,18},{3,1},{4,20},{5,7},{6,22},{7,5},{8,24},{9,11},... | collective-permute-start | bytes 2211848 | tf_op jit(solution)/shard_map/ppermute | solution.py:39
  85.6 26.8 %collective-permute-start.14 = (bf16[120,512]{1,0:T(8,128)(2,1)}, bf16[120,512]{1,0:T(8,128)(2,1)}, u32[]{:S(2)}, u32[]{:S(2)}) collective-permute-start(bf16[120,512]{1,0:T(8,128)(2,1)} %pad_maximum_fusion.15), channel_id=1, source_target_pairs={{0,4},{1,5},{2,6},{3,7},{4,8},{5,9},{6,10},{7,11},{8,12},{9,13},{1... | collective-permute-start | bytes 368648 | tf_op jit(solution)/shard_map/ppermute | solution.py:39
  88.6 25.4 %collective-permute-start.15 = (bf16[120,512]{1,0:T(8,128)(2,1)}, bf16[120,512]{1,0:T(8,128)(2,1)}, u32[]{:S(2)}, u32[]{:S(2)}) collective-permute-start(bf16[120,512]{1,0:T(8,128)(2,1)} %pad_maximum_fusion.15), channel_id=1, source_target_pairs={{0,8},{1,9},{2,10},{3,11},{4,12},{5,13},{6,14},{7,15},{8,0},{9,1},... | collective-permute-start | bytes 368648 | tf_op jit(solution)/shard_map/ppermute | solution.py:39
  103.8 12.0 %copy-start.34 = (bf16[960,512]{1,0:T(8,128)(2,1)}, bf16[960,512]{1,0:T(8,128)(2,1)S(1)}, u32[]{:S(2)}) copy-start(bf16[960,512]{1,0:T(8,128)(2,1)S(1)} %get-tuple-element.149.mixed_ref.refs_7_) | copy-start | bytes 2949124
  103.8 10.1 %collective-permute-start.16 = (bf16[120,512]{1,0:T(8,128)(2,1)}, bf16[120,512]{1,0:T(8,128)(2,1)S(1)}, u32[]{:S(2)}, u32[]{:S(2)}) collective-permute-start(bf16[120,512]{1,0:T(8,128)(2,1)} %pad_maximum_fusion.15), channel_id=1, source_target_pairs={{0,12},{1,13},{2,14},{3,15},{4,0},{5,1},{6,2},{7,3},{8,4},{9,5},{1... | collective-permute-start | bytes 368648 | tf_op jit(solution)/shard_map/ppermute | solution.py:39
  109.8 31.7 %collective-permute-start.23 = (bf16[4,2,160,960]{3,2,1,0:T(8,128)(2,1)}, bf16[4,2,160,960]{3,2,1,0:T(8,128)(2,1)}, u32[]{:S(2)}, u32[]{:S(2)}) collective-permute-start(bf16[4,2,160,960]{3,2,1,0:T(8,128)(2,1)} %bitcast.30.refs_5_), channel_id=1, source_target_pairs={{0,1},{1,0},{2,3},{3,2},{4,5},{5,4},{6,7},{7,6},{8,9},{9,8},{10,11... | collective-permute-start | bytes 7372808 | tf_op jit(solution)/shard_map/ppermute | solution.py:39
  112.4 24.9 %collective-permute-start.19 = (bf16[2,4,120,768]{3,2,1,0:T(8,128)(2,1)}, bf16[2,4,120,768]{3,2,1,0:T(8,128)(2,1)}, u32[]{:S(2)}, u32[]{:S(2)}) collective-permute-start(bf16[2,4,120,768]{3,2,1,0:T(8,128)(2,1)} %pad_maximum_fusion.held_ref), channel_id=1, source_target_pairs={{0,2},{1,17},{2,0},{3,19},{4,6},{5,21},{6,4},{7,23},{8,10},{9,25},... | collective-permute-start | bytes 4423688 | tf_op jit(solution)/shard_map/ppermute | solution.py:39
  118.8 21.0 %copy-start.29 = (bf16[960,512]{1,0:T(8,128)(2,1)}, bf16[960,512]{1,0:T(8,128)(2,1)S(1)}, u32[]{:S(2)}) copy-start(bf16[960,512]{1,0:T(8,128)(2,1)S(1)} %get-tuple-element.151.refs_0_) | copy-start | bytes 2949124
  118.8 22.7 %collective-permute-start.21 = (bf16[960,512]{1,0:T(8,128)(2,1)S(1)}, bf16[960,512]{1,0:T(8,128)(2,1)}, u32[]{:S(2)}, u32[]{:S(2)}) collective-permute-start(bf16[960,512]{1,0:T(8,128)(2,1)S(1)} %get-tuple-element.151.refs_0_), channel_id=1, source_target_pairs={{0,1},{1,0},{2,3},{3,2},{4,5},{5,4},{6,7},{7,6},{8,9},{9,8},{10,11... | collective-permute-start | bytes 2949128 | tf_op jit(solution)/shard_map/ppermute | solution.py:39
  118.8 14.5 %collective-permute-start.20 = (bf16[4,120,512]{2,1,0:T(8,128)(2,1)}, bf16[4,120,512]{2,1,0:T(8,128)(2,1)}, u32[]{:S(2)}, u32[]{:S(2)}) collective-permute-start(bf16[4,120,512]{2,1,0:T(8,128)(2,1)} %pad_maximum_fusion.12), channel_id=1, source_target_pairs={{0,16},{1,3},{2,18},{3,1},{4,20},{5,7},{6,22},{7,5},{8,24},{9,11},... | collective-permute-start | bytes 1474568 | tf_op jit(solution)/shard_map/ppermute | solution.py:39
  135.4 29.2 %collective-permute-start.24 = (bf16[2,4,120,512]{3,2,1,0:T(8,128)(2,1)}, bf16[2,4,120,512]{3,2,1,0:T(8,128)(2,1)}, u32[]{:S(2)}, u32[]{:S(2)}) collective-permute-start(bf16[2,4,120,512]{3,2,1,0:T(8,128)(2,1)} %pad_maximum_fusion.6.held_ref), channel_id=1, source_target_pairs={{0,2},{1,17},{2,0},{3,19},{4,6},{5,21},{6,4},{7,23},{8,10},{9,25},... | collective-permute-start | bytes 2949128 | tf_op jit(solution)/shard_map/ppermute | solution.py:39
  182.4 5.1 %collective-permute-start.28 = (bf16[960,512]{1,0:T(8,128)(2,1)}, bf16[960,512]{1,0:T(8,128)(2,1)}, u32[]{:S(2)}, u32[]{:S(2)}) collective-permute-start(bf16[960,512]{1,0:T(8,128)(2,1)} %get-tuple-element.176), channel_id=1, source_target_pairs={{0,1},{1,0},{2,3},{3,2},{4,5},{5,4},{6,7},{7,6},{8,9},{9,8},{10,11... | collective-permute-start | bytes 2949128 | tf_op jit(solution)/shard_map/ppermute | solution.py:39
  182.5 5.0 %collective-permute-start.27 = (bf16[960,512]{1,0:T(8,128)(2,1)S(1)}, bf16[960,512]{1,0:T(8,128)(2,1)}, u32[]{:S(2)}, u32[]{:S(2)}) collective-permute-start(bf16[960,512]{1,0:T(8,128)(2,1)S(1)} %get-tuple-element.174), channel_id=1, source_target_pairs={{0,1},{1,0},{2,3},{3,2},{4,5},{5,4},{6,7},{7,6},{8,9},{9,8},{10,11... | collective-permute-start | bytes 2949128 | tf_op jit(solution)/shard_map/ppermute | solution.py:39
  183.0 19.7 %collective-permute-start.29 = (bf16[2,4,120,768]{3,2,1,0:T(8,128)(2,1)}, bf16[2,4,120,768]{3,2,1,0:T(8,128)(2,1)}, u32[]{:S(2)}, u32[]{:S(2)}) collective-permute-start(bf16[2,4,120,768]{3,2,1,0:T(8,128)(2,1)} %pad_maximum_fusion.1), channel_id=1, source_target_pairs={{0,2},{1,17},{2,0},{3,19},{4,6},{5,21},{6,4},{7,23},{8,10},{9,25},... | collective-permute-start | bytes 4423688 | tf_op jit(solution)/shard_map/ppermute | solution.py:39
  186.9 32.2 %collective-permute-start.31 = (bf16[2,4,120,512]{3,2,1,0:T(8,128)(2,1)}, bf16[2,4,120,512]{3,2,1,0:T(8,128)(2,1)}, u32[]{:S(2)}, u32[]{:S(2)}) collective-permute-start(bf16[2,4,120,512]{3,2,1,0:T(8,128)(2,1)} %pad_maximum_fusion.7), channel_id=1, source_target_pairs={{0,2},{1,17},{2,0},{3,19},{4,6},{5,21},{6,4},{7,23},{8,10},{9,25},... | collective-permute-start | bytes 2949128 | tf_op jit(solution)/shard_map/ppermute | solution.py:39
  198.8 20.2 %copy-start.11 = (f32[960,512]{1,0:T(8,128)}, f32[960,512]{1,0:T(8,128)S(1)}, u32[]{:S(2)}) copy-start(f32[960,512]{1,0:T(8,128)S(1)} %get-tuple-element.197.grad_ref) | copy-start | bytes 5898244
  205.0 18.8 %collective-permute-start.30 = (bf16[4,120,768]{2,1,0:T(8,128)(2,1)}, bf16[4,120,768]{2,1,0:T(8,128)(2,1)}, u32[]{:S(2)}, u32[]{:S(2)}) collective-permute-start(bf16[4,120,768]{2,1,0:T(8,128)(2,1)} %fusion.4), channel_id=1, source_target_pairs={{0,16},{1,3},{2,18},{3,1},{4,20},{5,7},{6,22},{7,5},{8,24},{9,11},... | collective-permute-start | bytes 2211848 | tf_op jit(solution)/shard_map/ppermute | solution.py:39
  232.4 11.3 %collective-permute-start.32 = (bf16[960,1280]{1,0:T(8,128)(2,1)}, bf16[960,1280]{1,0:T(8,128)(2,1)}, u32[]{:S(2)}, u32[]{:S(2)}) collective-permute-start(bf16[960,1280]{1,0:T(8,128)(2,1)} %get-tuple-element.198), channel_id=1, source_target_pairs={{0,1},{1,0},{2,3},{3,2},{4,5},{5,4},{6,7},{7,6},{8,9},{9,8},{10,11... | collective-permute-start | bytes 7372808 | tf_op jit(solution)/shard_map/ppermute | solution.py:39
  232.5 23.2 %collective-permute-start.35 = (bf16[2,2,2,80,960]{4,3,2,1,0:T(8,128)(2,1)}, bf16[2,2,2,80,960]{4,3,2,1,0:T(8,128)(2,1)}, u32[]{:S(2)}, u32[]{:S(2)}) collective-permute-start(bf16[2,2,2,80,960]{4,3,2,1,0:T(8,128)(2,1)} %pad_maximum_fusion.3), channel_id=1, source_target_pairs={{0,2},{1,17},{2,0},{3,19},{4,6},{5,21},{6,4},{7,23},{8,10},{9,25},... | collective-permute-start | bytes 3686408 | tf_op jit(solution)/shard_map/ppermute | solution.py:39
  233.9 24.5 %collective-permute-start.34 = (bf16[4,120,512]{2,1,0:T(8,128)(2,1)}, bf16[4,120,512]{2,1,0:T(8,128)(2,1)S(1)}, u32[]{:S(2)}, u32[]{:S(2)}) collective-permute-start(bf16[4,120,512]{2,1,0:T(8,128)(2,1)} %fusion.16), channel_id=1, source_target_pairs={{0,16},{1,3},{2,18},{3,1},{4,20},{5,7},{6,22},{7,5},{8,24},{9,11},... | collective-permute-start | bytes 1474568 | tf_op jit(solution)/shard_map/ppermute | solution.py:39
  246.5 29.3 %collective-permute-start.33 = (bf16[2,4,120,640]{3,2,1,0:T(8,128)(2,1)}, bf16[2,4,120,640]{3,2,1,0:T(8,128)(2,1)}, u32[]{:S(2)}, u32[]{:S(2)}) collective-permute-start(bf16[2,4,120,640]{3,2,1,0:T(8,128)(2,1)} %pad_maximum_fusion.5), channel_id=1, source_target_pairs={{0,2},{1,17},{2,0},{3,19},{4,6},{5,21},{6,4},{7,23},{8,10},{9,25},... | collective-permute-start | bytes 3686408 | tf_op jit(solution)/shard_map/ppermute | solution.py:39
  247.4 46.7 %collective-permute-start.26 = (bf16[960,512]{1,0:T(8,128)(2,1)}, bf16[960,512]{1,0:T(8,128)(2,1)}, u32[]{:S(2)}, u32[]{:S(2)}) collective-permute-start(bf16[960,512]{1,0:T(8,128)(2,1)} %get-tuple-element.171), channel_id=1, source_target_pairs={{0,1},{1,0},{2,3},{3,2},{4,5},{5,4},{6,7},{7,6},{8,9},{9,8},{10,11... | collective-permute-start | bytes 2949128 | tf_op jit(solution)/shard_map/ppermute | solution.py:39
  257.2 23.2 %collective-permute-start.40 = (bf16[2,2,80,960]{3,2,1,0:T(8,128)(2,1)S(1)}, bf16[2,2,80,960]{3,2,1,0:T(8,128)(2,1)S(1)}, u32[]{:S(2)}, u32[]{:S(2)}) collective-permute-start(bf16[2,2,80,960]{3,2,1,0:T(8,128)(2,1)S(1)} %fusion.9), channel_id=1, source_target_pairs={{0,16},{1,3},{2,18},{3,1},{4,20},{5,7},{6,22},{7,5},{8,24},{9,11},... | collective-permute-start | bytes 1843208 | tf_op jit(solution)/shard_map/ppermute | solution.py:39
  259.9 18.2 %copy-start.10 = (bf16[960,1280]{1,0:T(8,128)(2,1)S(1)}, bf16[960,1280]{1,0:T(8,128)(2,1)}, u32[]{:S(2)}) copy-start(bf16[960,1280]{1,0:T(8,128)(2,1)} %copy-done.8) | copy-start | bytes 7372804
  260.0 22.0 %collective-permute-start.37 = (bf16[120,1280]{1,0:T(8,128)(2,1)S(1)}, bf16[120,1280]{1,0:T(8,128)(2,1)S(1)}, u32[]{:S(2)}, u32[]{:S(2)}) collective-permute-start(bf16[120,1280]{1,0:T(8,128)(2,1)S(1)} %get-tuple-element.230), channel_id=1, source_target_pairs={{0,4},{1,5},{2,6},{3,7},{4,8},{5,9},{6,10},{7,11},{8,12},{9,13},{1... | collective-permute-start | bytes 921608 | tf_op jit(solution)/shard_map/ppermute | solution.py:39
  260.6 23.5 %collective-permute-start.38 = (bf16[120,1280]{1,0:T(8,128)(2,1)S(1)}, bf16[120,1280]{1,0:T(8,128)(2,1)S(1)}, u32[]{:S(2)}, u32[]{:S(2)}) collective-permute-start(bf16[120,1280]{1,0:T(8,128)(2,1)S(1)} %get-tuple-element.229), channel_id=1, source_target_pairs={{0,8},{1,9},{2,10},{3,11},{4,12},{5,13},{6,14},{7,15},{8,0},{9,1},... | collective-permute-start | bytes 921608 | tf_op jit(solution)/shard_map/ppermute | solution.py:39
  275.8 14.1 %collective-permute-start.39 = (bf16[120,1280]{1,0:T(8,128)(2,1)S(1)}, bf16[120,1280]{1,0:T(8,128)(2,1)S(1)}, u32[]{:S(2)}, u32[]{:S(2)}) collective-permute-start(bf16[120,1280]{1,0:T(8,128)(2,1)S(1)} %get-tuple-element.228), channel_id=1, source_target_pairs={{0,12},{1,13},{2,14},{3,15},{4,0},{5,1},{6,2},{7,3},{8,4},{9,5},{1... | collective-permute-start | bytes 921608 | tf_op jit(solution)/shard_map/ppermute | solution.py:39
  280.4 13.7 %collective-permute-start.25 = (bf16[960,512]{1,0:T(8,128)(2,1)}, bf16[960,512]{1,0:T(8,128)(2,1)}, u32[]{:S(2)}, u32[]{:S(2)}) collective-permute-start(bf16[960,512]{1,0:T(8,128)(2,1)} %get-tuple-element.170), channel_id=1, source_target_pairs={{0,1},{1,0},{2,3},{3,2},{4,5},{5,4},{6,7},{7,6},{8,9},{9,8},{10,11... | collective-permute-start | bytes 2949128 | tf_op jit(solution)/shard_map/ppermute | solution.py:39
  291.9 12.3 %collective-permute-start.51 = (bf16[60,1280]{1,0:T(8,128)(2,1)S(1)}, bf16[60,1280]{1,0:T(8,128)(2,1)S(1)}, u32[]{:S(2)}, u32[]{:S(2)}) collective-permute-start(bf16[60,1280]{1,0:T(8,128)(2,1)S(1)} %get-tuple-element.261), channel_id=1, source_target_pairs={{0,1},{1,0},{2,3},{3,2},{4,5},{5,4},{6,7},{7,6},{8,9},{9,8},{10,11... | collective-permute-start | bytes 460808 | tf_op jit(solution)/shard_map/ppermute | solution.py:39
  291.9 13.5 %collective-permute-start.52 = (bf16[60,1280]{1,0:T(8,128)(2,1)S(1)}, bf16[60,1280]{1,0:T(8,128)(2,1)S(1)}, u32[]{:S(2)}, u32[]{:S(2)}) collective-permute-start(bf16[60,1280]{1,0:T(8,128)(2,1)S(1)} %get-tuple-element.261), channel_id=1, source_target_pairs={{0,17},{1,16},{2,19},{3,18},{4,21},{5,20},{6,23},{7,22},{8,25},{9,... | collective-permute-start | bytes 460808 | tf_op jit(solution)/shard_map/ppermute | solution.py:39
  292.9 9.9 %collective-permute-start.50 = (bf16[60,1280]{1,0:T(8,128)(2,1)S(1)}, bf16[60,1280]{1,0:T(8,128)(2,1)S(1)}, u32[]{:S(2)}, u32[]{:S(2)}) collective-permute-start(bf16[60,1280]{1,0:T(8,128)(2,1)S(1)} %bitcast.220), channel_id=1, source_target_pairs={{0,16},{1,17},{2,18},{3,19},{4,20},{5,21},{6,22},{7,23},{8,24},{9,... | collective-permute-start | bytes 460808 | tf_op jit(solution)/shard_map/ppermute | solution.py:39
  299.3 10.1 %collective-permute-start.36 = (bf16[4,120,640]{2,1,0:T(8,128)(2,1)S(1)}, bf16[4,120,640]{2,1,0:T(8,128)(2,1)S(1)}, u32[]{:S(2)}, u32[]{:S(2)}) collective-permute-start(bf16[4,120,640]{2,1,0:T(8,128)(2,1)S(1)} %copy-done.41), channel_id=1, source_target_pairs={{0,16},{1,3},{2,18},{3,1},{4,20},{5,7},{6,22},{7,5},{8,24},{9,11},... | collective-permute-start | bytes 1843208 | tf_op jit(solution)/shard_map/ppermute | solution.py:39
  300.3 14.3 %collective-permute-start.44 = (bf16[2,80,960]{2,1,0:T(8,128)(2,1)S(1)}, bf16[2,80,960]{2,1,0:T(8,128)(2,1)S(1)}, u32[]{:S(2)}, u32[]{:S(2)}) collective-permute-start(bf16[2,80,960]{2,1,0:T(8,128)(2,1)S(1)} %get-tuple-element.242), channel_id=1, source_target_pairs={{0,4},{2,6},{5,9},{7,11},{9,13},{11,15},{12,0},{14,2},{16,20},{18,... | collective-permute-start | bytes 921608 | tf_op jit(solution)/shard_map/ppermute | solution.py:235
  302.8 16.1 %collective-permute-start.45 = (bf16[2,80,960]{2,1,0:T(8,128)(2,1)S(1)}, bf16[2,80,960]{2,1,0:T(8,128)(2,1)S(1)}, u32[]{:S(2)}, u32[]{:S(2)}) collective-permute-start(bf16[2,80,960]{2,1,0:T(8,128)(2,1)S(1)} %get-tuple-element.241), channel_id=1, source_target_pairs={{1,9},{3,11},{5,13},{7,15},{8,0},{10,2},{12,4},{14,6},{17,25},{19,... | collective-permute-start | bytes 921608 | tf_op jit(solution)/shard_map/ppermute | solution.py:235
  304.1 14.8 %collective-permute-start.46 = (bf16[2,80,960]{2,1,0:T(8,128)(2,1)S(1)}, bf16[2,80,960]{2,1,0:T(8,128)(2,1)S(1)}, u32[]{:S(2)}, u32[]{:S(2)}) collective-permute-start(bf16[2,80,960]{2,1,0:T(8,128)(2,1)S(1)} %get-tuple-element.240), channel_id=1, source_target_pairs={{1,13},{3,15},{4,0},{6,2},{8,4},{10,6},{13,9},{15,11},{17,29},{19,... | collective-permute-start | bytes 921608 | tf_op jit(solution)/shard_map/ppermute | solution.py:235
  318.9 14.6 %collective-permute-start.41 = (bf16[120,640]{1,0:T(8,128)(2,1)S(1)}, bf16[120,640]{1,0:T(8,128)(2,1)S(1)}, u32[]{:S(2)}, u32[]{:S(2)}) collective-permute-start(bf16[120,640]{1,0:T(8,128)(2,1)S(1)} %get-tuple-element.254), channel_id=1, source_target_pairs={{0,4},{1,5},{2,6},{3,7},{4,8},{5,9},{6,10},{7,11},{8,12},{9,13},{1... | collective-permute-start | bytes 460808 | tf_op jit(solution)/shard_map/ppermute | solution.py:39
  330.8 7.2 %collective-permute-start.42 = (bf16[120,640]{1,0:T(8,128)(2,1)S(1)}, bf16[120,640]{1,0:T(8,128)(2,1)S(1)}, u32[]{:S(2)}, u32[]{:S(2)}) collective-permute-start(bf16[120,640]{1,0:T(8,128)(2,1)S(1)} %get-tuple-element.253), channel_id=1, source_target_pairs={{0,8},{1,9},{2,10},{3,11},{4,12},{5,13},{6,14},{7,15},{8,0},{9,1},... | collective-permute-start | bytes 460808 | tf_op jit(solution)/shard_map/ppermute | solution.py:39
  330.8 7.2 %collective-permute-start.43 = (bf16[120,640]{1,0:T(8,128)(2,1)S(1)}, bf16[120,640]{1,0:T(8,128)(2,1)S(1)}, u32[]{:S(2)}, u32[]{:S(2)}) collective-permute-start(bf16[120,640]{1,0:T(8,128)(2,1)S(1)} %get-tuple-element.252), channel_id=1, source_target_pairs={{0,12},{1,13},{2,14},{3,15},{4,0},{5,1},{6,2},{7,3},{8,4},{9,5},{1... | collective-permute-start | bytes 460808 | tf_op jit(solution)/shard_map/ppermute | solution.py:39
  333.4 7.0 %collective-permute-start.53 = (bf16[80,960]{1,0:T(8,128)(2,1)S(1)}, bf16[80,960]{1,0:T(8,128)(2,1)S(1)}, u32[]{:S(2)}, u32[]{:S(2)}) collective-permute-start(bf16[80,960]{1,0:T(8,128)(2,1)S(1)} %dynamic-slice_bitcast_fusion.14), channel_id=1, source_target_pairs={{0,1},{1,0},{2,3},{3,2},{4,5},{5,4},{6,7},{7,6},{8,9},{9,8},{10,11... | collective-permute-start | bytes 460808 | tf_op jit(solution)/shard_map/ppermute | solution.py:39
  338.2 7.2 %collective-permute-start.48 = (bf16[60,640]{1,0:T(8,128)(2,1)S(1)}, bf16[60,640]{1,0:T(8,128)(2,1)S(1)}, u32[]{:S(2)}, u32[]{:S(2)}) collective-permute-start(bf16[60,640]{1,0:T(8,128)(2,1)S(1)} %get-tuple-element.269), channel_id=1, source_target_pairs={{0,1},{1,0},{2,3},{3,2},{4,5},{5,4},{6,7},{7,6},{8,9},{9,8},{10,11... | collective-permute-start | bytes 230408 | tf_op jit(solution)/shard_map/ppermute | solution.py:39
  338.3 7.1 %collective-permute-start.49 = (bf16[60,640]{1,0:T(8,128)(2,1)S(1)}, bf16[60,640]{1,0:T(8,128)(2,1)S(1)}, u32[]{:S(2)}, u32[]{:S(2)}) collective-permute-start(bf16[60,640]{1,0:T(8,128)(2,1)S(1)} %get-tuple-element.269), channel_id=1, source_target_pairs={{0,17},{1,16},{2,19},{3,18},{4,21},{5,20},{6,23},{7,22},{8,25},{9,... | collective-permute-start | bytes 230408 | tf_op jit(solution)/shard_map/ppermute | solution.py:39
  339.6 5.8 %collective-permute-start.47 = (bf16[60,640]{1,0:T(8,128)(2,1)S(1)}, bf16[60,640]{1,0:T(8,128)(2,1)S(1)}, u32[]{:S(2)}, u32[]{:S(2)}) collective-permute-start(bf16[60,640]{1,0:T(8,128)(2,1)S(1)} %bitcast.225), channel_id=1, source_target_pairs={{0,16},{1,17},{2,18},{3,19},{4,20},{5,21},{6,22},{7,23},{8,24},{9,... | collective-permute-start | bytes 230408 | tf_op jit(solution)/shard_map/ppermute | solution.py:39
  340.5 7.9 %collective-permute-start.54 = (bf16[80,960]{1,0:T(8,128)(2,1)S(1)}, bf16[80,960]{1,0:T(8,128)(2,1)S(1)}, u32[]{:S(2)}, u32[]{:S(2)}) collective-permute-start(bf16[80,960]{1,0:T(8,128)(2,1)S(1)} %bitcast_select_fusion), channel_id=1, source_target_pairs={{0,16},{1,17},{2,18},{3,19},{4,20},{5,21},{6,22},{7,23},{8,24},{9,... | collective-permute-start | bytes 460808 | tf_op jit(solution)/shard_map/ppermute | solution.py:39
  (40 other events, 171.6 us)
